TPU v7x, 128 devices: a whole 4x4x4 slice. The times are simulated.
128 devices in a mesh: group: 2 (over y_hi), tile: 64 (over x, z, y_lo, core).
Axes of the slice: x: 4, y: 4 (y_hi: 2, y_lo: 2; y = y_hi * 2 + y_lo), z: 4, core: 2. Of those that a mesh axis runs over, the one named last changes fastest.
Arguments:
- site_tensors: bfloat16 [64, 6, 2, 65536], P('tile', 'group'), may hold values from -6 to 6
- msg_in: float32 [64, 6, 4, 256], P('tile', 'group'), may hold values from -6 to 6
Outputs:
- new_tensors: bfloat16 [64, 6, 2, 65536], P('tile', 'group')
- messages: float32 [64, 6, 4, 256], P('tile', 'group')
All inputs are finite; a program needn't handle non-finite values.
Results may differ from a plain program's by a relative error of at most 0.029.
The roundings to bfloat16 on the way count: a program that leaves them out, or rounds other values in their place, can miss the bound.
Values may be sent and summed in bfloat16 or wider, within the bound.
No kernel may reach another device: no remote copies, remote signals or barrier semaphores. Data moves between devices by JAX's collectives and lax.ppermute only.
A program may use at most 256 MiB of HBM per device.

v0:
```python
import math

import jax
import jax.numpy as jnp
from jax import lax
from jax.experimental import pallas as pl
from jax.experimental.pallas import tpu as pltpu
from jax.sharding import PartitionSpec as P

D = 16
SQ = D * D
SITES = 3
STATES = 2
ITERS = 2
NS_STEPS = 6
UP, LEFT, DOWN, RIGHT = range(4)
LEGS = (UP, DOWN, LEFT, RIGHT)
SLOTS = 8
WIDE = SLOTS * D

epsilon = 1e-06
coupling_step = 0.5
field_step = 0.3
f32 = jnp.float32
bf16 = jnp.bfloat16


def iota(shape, dim):
    return lax.broadcasted_iota(jnp.int32, shape, dim)


def where_ones(condition):
    return jnp.where(condition, 1.0, 0.0).astype(bf16)


def minor(index):
    return index & (D - 1)


def major(index):
    return index >> 4


def selector(row_part, lane_part, lanes):
    return where_ones(row_part(iota((SQ, lanes), 0)) == lane_part(iota((SQ, lanes), 1)))


def dot(left, right):
    return jnp.dot(left, right, preferred_element_type=f32)


def dot_first(left, right):
    return lax.dot_general(left, right, (((0,), (0,)), ((), ())), preferred_element_type=f32)


def dot_split(left, right):
    high = left.astype(bf16)
    low = (left - high.astype(f32)).astype(bf16)
    return dot(high, right) + dot(low, right)


def kron(rep, tile):
    return (rep.astype(f32)[:, None, :] * tile.astype(f32)[None, :, :]).astype(bf16).reshape(SQ, SQ)


def place():
    tile = lax.axis_index("tile")
    at_end = (tile == 0) | (tile == lax.axis_size("tile") - 1)
    return lax.axis_index("group") == 0, (tile & 1) == 0, at_end


def slot_of_lane():
    return major(iota((D, WIDE), 1))


def pack_of(blocks):
    slots = slot_of_lane()
    pack = jnp.zeros((D, WIDE), f32)
    for slot, block in enumerate(blocks):
        pack = jnp.where(slots == slot, block, pack)
    return pack


def packs_of(blocks):
    first_half, even, _ = place()
    near = [jnp.where(even, blocks[DOWN][i], blocks[UP][i]) for i in range(SITES)]
    far = [jnp.where(even, blocks[UP][i], blocks[DOWN][i]) for i in range(SITES)]
    side = jnp.where(first_half, blocks[RIGHT][2], blocks[LEFT][0])
    inner = [blocks[RIGHT][0], blocks[RIGHT][1], blocks[LEFT][1], blocks[LEFT][2]]
    return pack_of(near + inner), pack_of(far + [side])


def rep(pack, slot):
    lane = iota((D, WIDE), 1)
    return jnp.concatenate(
        [
            jnp.take_along_axis(pack, slot * D + half * SLOTS + major(lane), axis=1)
            for half in range(2)
        ],
        axis=1,
    )


def tile(pack, slot):
    part = jnp.take_along_axis(pack, slot * D + minor(iota((D, WIDE), 1)), axis=1)
    return jnp.concatenate([part, part], axis=1)


def site_parts(a_ref, at_ref, site, up, left, down, right, split_states):
    parts = {leg: [] for leg in LEGS}
    for first, second, m_rep, m_tile, k_rep, k_tile, leg_rep, leg_tile in (
        (a_ref, at_ref, up, left, down, right, UP, LEFT),
        (at_ref, a_ref, down, right, up, left, DOWN, RIGHT),
    ):
        weight = kron(k_rep, k_tile)
        kept = [dot(first[site, s], weight).astype(bf16) for s in range(STATES)]
        products = [dot(kept[s], second[site, s]) for s in range(STATES)]
        if not split_states:
            products = [products[0] + products[1]]
        for product in products:
            cube = product.reshape(D, D, SQ)
            parts[leg_rep].append(jnp.sum(cube * m_tile[None, :, :], axis=1))
            parts[leg_tile].append(jnp.sum(cube * m_rep[:, None, :], axis=0))
    return parts


def finish(parts, split_states):
    count = STATES if split_states else 1
    results = [{}, {}]
    for legs, pick in (
        ((UP, DOWN), selector(major, minor, WIDE)),
        ((LEFT, RIGHT), selector(minor, minor, WIDE)),
    ):
        rows = [parts[site][leg][s] for leg in legs for site in range(SITES) for s in range(count)]
        blocks = dot_split(jnp.concatenate(rows, axis=0), pick).reshape(2, SITES, count, D, WIDE)
        for index, leg in enumerate(legs):
            block = blocks[index]
            summed = block[:, 0] + block[:, 1] if split_states else block[:, 0]
            mean = jnp.mean(summed * summed, axis=(1, 2), keepdims=True)
            inverse = 1.0 / jnp.sqrt(mean + epsilon)
            results[0][leg] = summed * inverse
            if split_states:
                results[1][leg] = (block[:, 0] - block[:, 1]) * inverse
    return results


def leg_rows(msg, leg):
    return jnp.concatenate([msg[site, leg : leg + 1] for site in range(SITES)], axis=0)


def first_kernel(
    x_ref, msg_ref, a_ref, at_ref, edge_ref, near_ref, far_ref, x_buf, msg_buf, wide_ref, sems
):
    copies = [
        pltpu.make_async_copy(x_ref.at[site], x_buf.at[site], sems.at[site])
        for site in range(SITES)
    ]
    msg_copy = pltpu.make_async_copy(msg_ref, msg_buf, sems.at[SITES])
    msg_copy.start()
    for copy in copies:
        copy.start()
    msg_copy.wait()
    msg = msg_buf[...]
    rows = jnp.concatenate([leg_rows(msg, leg) for leg in LEGS], axis=0)
    count = rows.shape[0]
    keep = iota((count, D, SQ), 1) == major(iota((count, D, SQ), 2))
    spread = jnp.broadcast_to(rows[:, None, :], (count, D, SQ))
    spread = jnp.where(keep, spread, 0.0).reshape(count * D, SQ)
    ends = dot(spread[: count // 2 * D].astype(bf16), selector(minor, major, SQ))
    sides = dot(spread[count // 2 * D :].astype(bf16), selector(minor, minor, SQ))
    ends, sides = (both.reshape(2, SITES, D, SQ) for both in (ends, sides))
    exact = dot_split(spread, selector(minor, minor, WIDE)).reshape(4, SITES, D, WIDE)
    first_half, even, _ = place()
    outer = jnp.where(first_half, exact[2, 0], exact[3, 2])
    edges = [jnp.where(even, exact[0, i], exact[1, i]) for i in range(SITES)]
    edge_ref[...] = pack_of(edges + [outer])
    parts = []
    for site in range(SITES):
        copies[site].wait()
        wide_ref[site] = x_buf[site].astype(f32)
        for s in range(STATES):
            halves = [wide_ref[site, pl.ds(2 * half + s, SQ, stride=4), :] for half in range(2)]
            block = jnp.concatenate(halves, axis=1)
            a_ref[site, s] = block.astype(bf16)
            at_ref[site, s] = block.T.astype(bf16)
        parts.append(
            site_parts(
                a_ref, at_ref, site,
                ends[0, site], sides[0, site], ends[1, site], sides[1, site], False,
            )
        )
    out, _ = finish(parts, False)
    near_ref[...], far_ref[...] = packs_of(out)


def incoming_packs(near_own, edge, near_in, far_in, side_in):
    first_half, even, at_end = place()
    far = jnp.where(at_end, edge, far_in)
    up = jnp.where(even, far, near_in)
    down = jnp.where(even, near_in, far)
    left_end = jnp.where(first_half, edge, side_in)
    right_end = jnp.where(first_half, side_in, edge)
    return {
        UP: [(up, 0), (up, 1), (up, 2)],
        DOWN: [(down, 0), (down, 1), (down, 2)],
        LEFT: [(left_end, 3), (near_own, 3), (near_own, 4)],
        RIGHT: [(near_own, 5), (near_own, 6), (right_end, 3)],
    }


def second_kernel(
    a_ref, at_ref, edge_ref, near_own, near_in, far_in, side_in, near_ref, far_ref
):
    def rounded(ref):
        return ref[...].astype(bf16).astype(f32)

    where = incoming_packs(*(rounded(ref) for ref in (near_own, edge_ref, near_in, far_in, side_in)))
    parts = []
    for site in range(SITES):
        forms = [
            (rep if leg in (UP, DOWN) else tile)(*where[leg][site]) for leg in range(4)
        ]
        parts.append(site_parts(a_ref, at_ref, site, *forms, True))
    for index, values in enumerate(finish(parts, True)):
        near, far = packs_of(values)
        near_ref[index * D : index * D + D] = near
        far_ref[index * D : index * D + D] = far


def sum_of(terms):
    while len(terms) > 1:
        terms = [sum(terms[i : i + 2][1:], terms[i]) for i in range(0, len(terms), 2)]
    return terms[0]


def columns_of(pack):
    base = iota((D, WIDE), 1) & -D
    return [jnp.take_along_axis(pack, base + k, axis=1) for k in range(D)]


def times(columns, right):
    return sum_of([columns[k] * right[k : k + 1, :] for k in range(D)])


def inverse_root(power, eye):
    inverse = None
    for step in range(NS_STEPS):
        if inverse is None:
            following = 1.5 * eye - 0.5 * power
        columns = columns_of(power)
        if inverse is not None:
            following = 1.5 * inverse - 0.5 * times(columns, inverse)
        if step < NS_STEPS - 1:
            square = times(columns, power)
            power = 2.25 * power - 1.5 * square + 0.25 * times(columns, square)
        inverse = following
    return inverse


def bond_weights(both, both_twist, edge_lanes):
    weight_zero = math.cosh(coupling_step)
    weight_one = math.sinh(coupling_step)
    cross_weight = math.sqrt(weight_zero * weight_one)
    half_root = 1.0 / math.sqrt(2.0)
    top = ((weight_zero * both + cross_weight * both_twist) * half_root).astype(bf16).astype(f32)
    bottom = ((cross_weight * both_twist + weight_one * both) * half_root).astype(bf16).astype(f32)
    stacked = jnp.concatenate([top, bottom], axis=0).astype(bf16)
    inside = major(iota((WIDE, WIDE), 0)) == major(iota((WIDE, WIDE), 1))

    def packed(full):
        return jnp.sum(jnp.where(inside, full, 0.0).reshape(SLOTS, D, WIDE), axis=0)

    gram = packed(dot_first(stacked, stacked))
    squares = jnp.sum(top * top + bottom * bottom, axis=0, keepdims=True)
    squares = jnp.broadcast_to(squares, (D, WIDE))
    trace = dot_split(squares, where_ones(inside)) + epsilon
    identity = jnp.where(iota((D, WIDE), 0) == minor(iota((D, WIDE), 1)), 1.0, 0.0)
    inverse = inverse_root(gram / trace, identity).astype(bf16).astype(f32)
    spread = where_ones(iota((D, WIDE), 0) == minor(iota((D, WIDE), 1)))
    top_t, bottom_t = (packed(dot_first(half.astype(bf16), spread)) for half in (top, bottom))
    columns = columns_of(inverse)
    root = 1.0 / jnp.sqrt(trace)
    results = []
    for q_top, q_bottom in (
        (times(columns_of(top), inverse), times(columns_of(bottom), inverse)),
        (times(columns, top_t), times(columns, bottom_t)),
    ):
        first = math.sqrt(weight_zero) * (q_top * root)
        second = math.sqrt(weight_one) * (q_bottom * root)
        results.append(
            [
                jnp.where(edge_lanes, identity, weight).astype(bf16).astype(f32)
                for weight in (first + second, first - second)
            ]
        )
    return results


def early_kernel(a_ref, near_own, near_in, gated_ref, near_ref, inner_ref):
    _, even, _ = place()
    slots = slot_of_lane()
    other = (iota((D, WIDE), 1) + 2 * D) & (WIDE - 1)
    both = []
    for index in range(2):
        own = near_own[index * D : index * D + D]
        mate = jnp.take_along_axis(own, other, axis=1)
        mate = jnp.where(slots < 3, near_in[index * D : index * D + D], mate)
        both.append(jnp.where(slots < 5, own + mate, 0.0))
    grow, mix = math.cosh(field_step), math.sinh(field_step)
    for site in range(SITES):
        tensors = [a_ref[site, s].astype(f32) for s in range(STATES)]
        for s in range(STATES):
            gated_ref[site, s] = (grow * tensors[s] + mix * tensors[1 - s]).astype(bf16)
    plain, flipped = bond_weights(*both, slots < 0)
    for s in range(STATES):
        near = jnp.where(even, plain[s], flipped[s])
        for site in range(SITES):
            near_ref[s, site] = rep(near, site).astype(bf16)
        for index in range(2):
            inner_ref[s, 0, index] = tile(plain[s], 3 + index).astype(bf16)
            inner_ref[s, 1, index] = tile(flipped[s], 3 + index).astype(bf16)


def last_kernel(
    gated_ref, near_ref, inner_ref, edge_ref, near_own, far_own, near_in, far_in, side_in,
    x_ref, messages_ref, x_buf, msg_buf, wide_ref, sems,
):
    first_half, even, at_end = place()
    slots = slot_of_lane()
    both = []
    for index in range(2):
        part = slice(index * D, index * D + D)
        mate = jnp.where(slots < 3, far_in[part], side_in[part])
        both.append(jnp.where(slots < 4, far_own[part] + mate, 0.0))
    plain, flipped = bond_weights(*both, (slots < 3) & at_end)
    identity = where_ones(iota((D, SQ), 0) == minor(iota((D, SQ), 1)))
    factors = []
    for s in range(STATES):
        far_pack = jnp.where(even, flipped[s], plain[s])
        side = tile(jnp.where(first_half, plain[s], flipped[s]), 3).astype(bf16)
        far = [rep(far_pack, site).astype(bf16) for site in range(SITES)]
        near = [near_ref[s, site] for site in range(SITES)]
        ups = [jnp.where(even, far[i], near[i]) for i in range(SITES)]
        downs = [jnp.where(even, near[i], far[i]) for i in range(SITES)]
        lefts = [jnp.where(first_half, identity, side), inner_ref[s, 1, 0], inner_ref[s, 1, 1]]
        rights = [inner_ref[s, 0, 0], inner_ref[s, 0, 1], jnp.where(first_half, side, identity)]
        factors.append((ups, downs, lefts, rights))
    where = incoming_packs(
        near_own[:D], edge_ref[...], near_in[:D], far_in[:D], side_in[:D]
    )
    own_row = iota((D, SQ), 0) == major(iota((D, SQ), 1))
    for leg in LEGS:
        for site in range(SITES):
            spread = jnp.where(own_row, tile(*where[leg][site]), 0.0)
            msg_buf[site, leg : leg + 1] = jnp.sum(spread, axis=0, keepdims=True)
    msg_copy = pltpu.make_async_copy(msg_buf, messages_ref, sems.at[SITES])
    msg_copy.start()
    copies = []
    for site in range(SITES):
        for s in range(STATES):
            ups, downs, lefts, rights = factors[s]
            upper = kron(ups[site], lefts[site])
            lower = kron(downs[site], rights[site])
            gated = dot(upper, gated_ref[site, s]).astype(bf16)
            gated = dot(gated, lower)
            for half in range(2):
                lanes = gated[:, half * 128 : half * 128 + 128]
                wide_ref[site, pl.ds(2 * half + s, SQ, stride=4), :] = lanes
        x_buf[site] = wide_ref[site].astype(bf16)
        copies.append(pltpu.make_async_copy(x_buf.at[site], x_ref.at[site], sems.at[site]))
        copies[site].start()
    for copy in copies:
        copy.wait()
    msg_copy.wait()


def call(kernel, outs, scratch=(), in_specs=None, out_specs=None):
    specs = {}
    if in_specs is not None:
        specs["in_specs"] = in_specs
    if out_specs is not None:
        specs["out_specs"] = out_specs
    return pl.pallas_call(
        kernel,
        out_shape=[jax.ShapeDtypeStruct(shape, dtype) for shape, dtype in outs],
        scratch_shapes=list(scratch),
        compiler_params=pltpu.CompilerParams(vmem_limit_bytes=40 * 2**20),
        **specs,
    )


def swap_near(value):
    count = lax.axis_size("tile")
    return lax.ppermute(value, "tile", [(i, i ^ 1) for i in range(count)])


def swap_far(value):
    count = lax.axis_size("tile")
    return lax.ppermute(value, "tile", [(i, (((i + 1) ^ 1) - 1) % count) for i in range(count)])


def swap_side(value):
    return lax.ppermute(value, "group", [(0, 1), (1, 0)])


def exchange(near, far):
    return swap_near(near), swap_far(far), swap_side(far)


def per_device(site_tensors, msg_in):
    x = site_tensors.reshape(SITES, STATES, 2 * SQ, 128)
    x = x.transpose(0, 2, 1, 3).reshape(SITES, 4 * SQ, 128)
    x = pltpu.with_memory_space_constraint(x, pltpu.HBM)
    msg = pltpu.with_memory_space_constraint(msg_in[0], pltpu.HBM)
    flat = ((SITES, 4 * SQ, 128), bf16)
    tensor = ((SITES, STATES, SQ, SQ), bf16)
    messages = ((SITES, 4, SQ), f32)
    pack = ((D, WIDE), f32)
    packs = ((2 * D, WIDE), f32)
    in_hbm = [pl.BlockSpec(memory_space=pltpu.HBM)] * 2
    scratch = [
        pltpu.VMEM(*flat),
        pltpu.VMEM(*messages),
        pltpu.VMEM((SITES, 4 * SQ, 128), f32),
        pltpu.SemaphoreType.DMA((SITES + 1,)),
    ]
    a, at, edges, near, far = call(
        first_kernel, [tensor, tensor, pack, pack, pack], scratch, in_specs=in_hbm
    )(x, msg)
    near, far = call(second_kernel, [packs, packs])(a, at, edges, near, *exchange(near, far))
    received = exchange(near, far)
    spread = ((STATES, SITES, D, SQ), bf16)
    inner = ((STATES, 2, 2, D, SQ), bf16)
    early = call(early_kernel, [tensor, spread, inner])(a, near, received[0])
    x, messages = call(last_kernel, [flat, messages], scratch, out_specs=in_hbm)(
        *early, edges, near, far, *received
    )
    x = x.reshape(SITES, 2 * SQ, STATES, 128).transpose(0, 2, 1, 3)
    return x.reshape(1, SITES, STATES, SQ * SQ), messages[None]


def solution(mesh):
    spec = P("tile", "group", None, None)
    return jax.shard_map(
        per_device, mesh=mesh, in_specs=(spec, spec), out_specs=(spec, spec), check_vma=False
    )
```

profile of v0, /device:TPU:0, one launch (start us, length us, event | category | flops | bytes accessed | tf_op | source)
XLA Modules:
  0.0 29.2 jit_solution(7721432839463888061)
XLA Ops:
  0.6 3.3 %shard_map.41 = (bf16[3,2,256,256]{3,2,1,0:T(8,128)(2,1)S(1)}, bf16[3,2,256,256]{3,2,1,0:T(8,128)(2,1)S(1)}, f32[16,128]{1,0:T(8,128)S(1)}, f32[16,128]{1,0:T(8,128)S(1)}, f32[16,128]{1,0:T(8,128)S(1)}) custom-call(bf16[3,1024,128]{2,1,0:T(8,128)(2,1)} %bitcast.12, f32[3,4,256]{2,1,0:T(4,128)} %bitcast.13), custom_call_target="tpu_custom_call" | custom-call | tf_op jit(solution)/shard_map/pallas_call | solution.py:427
  3.9 0.1 collective-permute-start
  4.0 3.4 %collective-permute-start.2 = (f32[16,128]{1,0:T(8,128)S(1)}, f32[16,128]{1,0:T(8,128)S(1)}, u32[]{:S(2)}, u32[]{:S(2)}) collective-permute-start(f32[16,128]{1,0:T(8,128)S(1)} %get-tuple-element.18), channel_id=1, source_target_pairs={{0,64},{64,0},{1,65},{65,1},{2,66},{66,2},{3,67},{67,3},{4,68},{68... | collective-permute-start | bytes 24584 | tf_op jit(solution)/shard_map/ppermute | solution.py:403
  7.4 6.1 %collective-permute-start.1 = (f32[16,128]{1,0:T(8,128)S(1)}, f32[16,128]{1,0:T(8,128)S(1)}, u32[]{:S(2)}, u32[]{:S(2)}) collective-permute-start(f32[16,128]{1,0:T(8,128)S(1)} %get-tuple-element.18), channel_id=1, source_target_pairs={{0,63},{1,2},{2,1},{3,4},{4,3},{5,6},{6,5},{7,8},{8,7},{9,10},{10,... | collective-permute-start | bytes 24584 | tf_op jit(solution)/shard_map/ppermute | solution.py:399
  13.5 0.0 collective-permute-done.near_in
  13.5 0.0 collective-permute-done.2.side_in
  13.5 1.4 %collective-permute-done.1.far_in = f32[16,128]{1,0:T(8,128)S(1)} collective-permute-done((f32[16,128]{1,0:T(8,128)S(1)}, f32[16,128]{1,0:T(8,128)S(1)}, u32[]{:S(2)}, u32[]{:S(2)}) %collective-permute-start.1) | collective-permute-done | bytes 8224 | tf_op jit(solution)/shard_map/ppermute | solution.py:399
  14.8 2.1 %shard_map.42 = (f32[32,128]{1,0:T(8,128)S(1)}, f32[32,128]{1,0:T(8,128)S(1)}) custom-call(bf16[3,2,256,256]{3,2,1,0:T(8,128)(2,1)S(1)} %get-tuple-element.14.a_ref, bf16[3,2,256,256]{3,2,1,0:T(8,128)(2,1)S(1)} %get-tuple-element.15.at_ref, f32[16,128]{1,0:T(8,128)S(1)} %get-tuple-element.16.edge_ref, f32[16,128]{1,0:T(8,128)S(1)} %get-tuple-element.17.near_own, ...), custom_call_target="tpu_custom_call" | custom-call | tf_op jit(solution)/shard_map/pallas_call | solution.py:430
  17.0 0.1 collective-permute-start.3
  17.1 1.9 %collective-permute-start.5 = (f32[32,128]{1,0:T(8,128)S(1)}, f32[32,128]{1,0:T(8,128)S(1)}, u32[]{:S(2)}, u32[]{:S(2)}) collective-permute-start(f32[32,128]{1,0:T(8,128)S(1)} %get-tuple-element.23.far_own), channel_id=1, source_target_pairs={{0,64},{64,0},{1,65},{65,1},{2,66},{66,2},{3,67},{67,3},{4,68},{68... | collective-permute-start | bytes 49160 | tf_op jit(solution)/shard_map/ppermute | solution.py:403
  19.0 5.0 %collective-permute-start.4 = (f32[32,128]{1,0:T(8,128)S(1)}, f32[32,128]{1,0:T(8,128)S(1)}, u32[]{:S(2)}, u32[]{:S(2)}) collective-permute-start(f32[32,128]{1,0:T(8,128)S(1)} %get-tuple-element.23.far_own), channel_id=1, source_target_pairs={{0,63},{1,2},{2,1},{3,4},{4,3},{5,6},{6,5},{7,8},{8,7},{9,10},{10,... | collective-permute-start | bytes 49160 | tf_op jit(solution)/shard_map/ppermute | solution.py:399
  24.0 0.0 collective-permute-done.3.near_in
  24.0 1.8 %shard_map.43 = (bf16[3,2,256,256]{3,2,1,0:T(8,128)(2,1)S(1)}, bf16[2,3,16,256]{3,2,1,0:T(8,128)(2,1)S(1)}, bf16[2,2,2,16,256]{4,3,2,1,0:T(8,128)(2,1)S(1)}) custom-call(bf16[3,2,256,256]{3,2,1,0:T(8,128)(2,1)S(1)} %get-tuple-element.14.a_ref, f32[32,128]{1,0:T(8,128)S(1)} %get-tuple-element.19.near_own, f32[32,128]{1,0:T(8,128)S(1)} %collective-permute-done.3.near_in), custom_call_target="tpu_custom_call" | custom-call | tf_op jit(solution)/shard_map/pallas_call | solution.py:434
  25.8 0.0 collective-permute-done.5.side_in
  25.8 0.6 %collective-permute-done.4.far_in = f32[32,128]{1,0:T(8,128)S(1)} collective-permute-done((f32[32,128]{1,0:T(8,128)S(1)}, f32[32,128]{1,0:T(8,128)S(1)}, u32[]{:S(2)}, u32[]{:S(2)}) %collective-permute-start.4) | collective-permute-done | bytes 16416 | tf_op jit(solution)/shard_map/ppermute | solution.py:399
  26.4 2.9 %shard_map.44 = (bf16[3,1024,128]{2,1,0:T(8,128)(2,1)}, f32[3,4,256]{2,1,0:T(4,128)}) custom-call(bf16[3,2,256,256]{3,2,1,0:T(8,128)(2,1)S(1)} %get-tuple-element.20.gated_ref, bf16[2,3,16,256]{3,2,1,0:T(8,128)(2,1)S(1)} %get-tuple-element.21.near_ref, bf16[2,2,2,16,256]{4,3,2,1,0:T(8,128)(2,1)S(1)} %get-tuple-element.22.inner_ref, ...), custom_call_target="tpu_custom_call" | custom-call | tf_op jit(solution)/shard_map/pallas_call | solution.py:435
Async XLA Ops:
  3.9 9.6 %collective-permute-start = (f32[16,128]{1,0:T(8,128)S(1)}, f32[16,128]{1,0:T(8,128)S(1)}, u32[]{:S(2)}, u32[]{:S(2)}) collective-permute-start(f32[16,128]{1,0:T(8,128)S(1)} %get-tuple-element.17.near_own), channel_id=1, source_target_pairs={{0,1},{1,0},{2,3},{3,2},{4,5},{5,4},{6,7},{7,6},{8,9},{9,8},{10,11... | collective-permute-start | bytes 24584 | tf_op jit(solution)/shard_map/ppermute | solution.py:394
  4.0 9.5 %collective-permute-start.2 = (f32[16,128]{1,0:T(8,128)S(1)}, f32[16,128]{1,0:T(8,128)S(1)}, u32[]{:S(2)}, u32[]{:S(2)}) collective-permute-start(f32[16,128]{1,0:T(8,128)S(1)} %get-tuple-element.18), channel_id=1, source_target_pairs={{0,64},{64,0},{1,65},{65,1},{2,66},{66,2},{3,67},{67,3},{4,68},{68... | collective-permute-start | bytes 24584 | tf_op jit(solution)/shard_map/ppermute | solution.py:403
  7.4 7.5 %collective-permute-start.1 = (f32[16,128]{1,0:T(8,128)S(1)}, f32[16,128]{1,0:T(8,128)S(1)}, u32[]{:S(2)}, u32[]{:S(2)}) collective-permute-start(f32[16,128]{1,0:T(8,128)S(1)} %get-tuple-element.18), channel_id=1, source_target_pairs={{0,63},{1,2},{2,1},{3,4},{4,3},{5,6},{6,5},{7,8},{8,7},{9,10},{10,... | collective-permute-start | bytes 24584 | tf_op jit(solution)/shard_map/ppermute | solution.py:399
  17.0 7.1 %collective-permute-start.3 = (f32[32,128]{1,0:T(8,128)S(1)}, f32[32,128]{1,0:T(8,128)S(1)}, u32[]{:S(2)}, u32[]{:S(2)}) collective-permute-start(f32[32,128]{1,0:T(8,128)S(1)} %get-tuple-element.19.near_own), channel_id=1, source_target_pairs={{0,1},{1,0},{2,3},{3,2},{4,5},{5,4},{6,7},{7,6},{8,9},{9,8},{10,11... | collective-permute-start | bytes 49160 | tf_op jit(solution)/shard_map/ppermute | solution.py:394
  17.1 8.7 %collective-permute-start.5 = (f32[32,128]{1,0:T(8,128)S(1)}, f32[32,128]{1,0:T(8,128)S(1)}, u32[]{:S(2)}, u32[]{:S(2)}) collective-permute-start(f32[32,128]{1,0:T(8,128)S(1)} %get-tuple-element.23.far_own), channel_id=1, source_target_pairs={{0,64},{64,0},{1,65},{65,1},{2,66},{66,2},{3,67},{67,3},{4,68},{68... | collective-permute-start | bytes 49160 | tf_op jit(solution)/shard_map/ppermute | solution.py:403
  19.0 7.4 %collective-permute-start.4 = (f32[32,128]{1,0:T(8,128)S(1)}, f32[32,128]{1,0:T(8,128)S(1)}, u32[]{:S(2)}, u32[]{:S(2)}) collective-permute-start(f32[32,128]{1,0:T(8,128)S(1)} %get-tuple-element.23.far_own), channel_id=1, source_target_pairs={{0,63},{1,2},{2,1},{3,4},{4,3},{5,6},{6,5},{7,8},{8,7},{9,10},{10,... | collective-permute-start | bytes 49160 | tf_op jit(solution)/shard_map/ppermute | solution.py:399
where the time goes:
time: 29.4 us; the launch traced here: 29.2 us
  starting transfers between devices  16.6 us (56%)
  Pallas kernels  10 us (34%)
  waiting for transfers between devices  1.93 us (7%)
  between operations  0.68 us (2%)
    ppermute x2, starting transfers between devices, swap_far(): lax.ppermute(value, 'tile', [(i, ((i + 1 ^ 1) - 1) % count) for i in rang...  11.1 us
    ppermute x2, starting transfers between devices, swap_side(): return lax.ppermute(value, 'group', [(0, 1), (1, 0)])  5.27 us
    pallas_call x1, Pallas kernels, per_device(): call(first_kernel, [tensor, tensor, pack, pack, pack], scratch, in_specs=...  3.28 us
    pallas_call x1, Pallas kernels, per_device(): call(last_kernel, [flat, messages], scratch, out_specs=in_hbm)  2.88 us
    pallas_call x1, Pallas kernels, per_device(): call(second_kernel, [packs, packs])  2.12 us
    ppermute x2, waiting for transfers between devices, swap_far(): lax.ppermute(value, 'tile', [(i, ((i + 1 ^ 1) - 1) % count) for i in rang...  1.92 us
    pallas_call x1, Pallas kernels, per_device(): early = call(early_kernel, [tensor, spread, inner])(a, near, received[0])  1.77 us
  transfers between devices with their start and end apart: 6, of which 2 were waited for; matrix products, arithmetic and copies ran while one was open for 0% of the time, Pallas kernels for 6%

commit v1 on v0

--- a/solution.py
+++ b/solution.py
@@ -149,7 +149,8 @@
 
 
 def first_kernel(
-    x_ref, msg_ref, a_ref, at_ref, edge_ref, near_ref, far_ref, x_buf, msg_buf, wide_ref, sems
+    x_ref, msg_ref, a_ref, at_ref, edge_ref, own_ref, near_ref, far_ref, side_ref,
+    x_buf, msg_buf, wide_ref, sems,
 ):
     copies = [
         pltpu.make_async_copy(x_ref.at[site], x_buf.at[site], sems.at[site])
@@ -175,8 +176,9 @@
     edges = [jnp.where(even, exact[0, i], exact[1, i]) for i in range(SITES)]
     edge_ref[...] = pack_of(edges + [outer])
     parts = []
+    for copy in copies:
+        copy.wait()
     for site in range(SITES):
-        copies[site].wait()
         wide_ref[site] = x_buf[site].astype(f32)
         for s in range(STATES):
             halves = [wide_ref[site, pl.ds(2 * half + s, SQ, stride=4), :] for half in range(2)]
@@ -190,7 +192,11 @@
             )
         )
     out, _ = finish(parts, False)
-    near_ref[...], far_ref[...] = packs_of(out)
+    near, far = packs_of(out)
+    own_ref[...] = near
+    near_ref[...] = near
+    far_ref[...] = far
+    side_ref[...] = far
 
 
 def incoming_packs(near_own, edge, near_in, far_in, side_in):
@@ -209,7 +215,8 @@
 
 
 def second_kernel(
-    a_ref, at_ref, edge_ref, near_own, near_in, far_in, side_in, near_ref, far_ref
+    a_ref, at_ref, edge_ref, near_own, near_in, far_in, side_in,
+    own_near_ref, own_far_ref, near_ref, far_ref, side_ref,
 ):
     def rounded(ref):
         return ref[...].astype(bf16).astype(f32)
@@ -223,8 +230,12 @@
         parts.append(site_parts(a_ref, at_ref, site, *forms, True))
     for index, values in enumerate(finish(parts, True)):
         near, far = packs_of(values)
-        near_ref[index * D : index * D + D] = near
-        far_ref[index * D : index * D + D] = far
+        part = slice(index * D, index * D + D)
+        own_near_ref[part] = near
+        own_far_ref[part] = far
+        near_ref[part] = near
+        far_ref[part] = far
+        side_ref[part] = far
 
 
 def sum_of(terms):
@@ -403,8 +414,8 @@
     return lax.ppermute(value, "group", [(0, 1), (1, 0)])
 
 
-def exchange(near, far):
-    return swap_near(near), swap_far(far), swap_side(far)
+def exchange(near, far, side):
+    return swap_near(near), swap_far(far), swap_side(side)
 
 
 def per_device(site_tensors, msg_in):
@@ -424,11 +435,11 @@
         pltpu.VMEM((SITES, 4 * SQ, 128), f32),
         pltpu.SemaphoreType.DMA((SITES + 1,)),
     ]
-    a, at, edges, near, far = call(
-        first_kernel, [tensor, tensor, pack, pack, pack], scratch, in_specs=in_hbm
+    a, at, edges, own, *parts = call(
+        first_kernel, [tensor, tensor, pack, pack, pack, pack, pack], scratch, in_specs=in_hbm
     )(x, msg)
-    near, far = call(second_kernel, [packs, packs])(a, at, edges, near, *exchange(near, far))
-    received = exchange(near, far)
+    near, far, *parts = call(second_kernel, [packs] * 5)(a, at, edges, own, *exchange(*parts))
+    received = exchange(*parts)
     spread = ((STATES, SITES, D, SQ), bf16)
     inner = ((STATES, 2, 2, D, SQ), bf16)
     early = call(early_kernel, [tensor, spread, inner])(a, near, received[0])

time: 29.4 us -> 28.8 us (0.980)
  starting transfers between devices: 16.6 us -> 15.6 us
  waiting for transfers between devices: 1.93 us -> 2.82 us
  Pallas kernels: 10 us -> 9.51 us
    ppermute x2, waiting for transfers between devices: 0.01 us -> 2.25 us  [swap_side(): return lax.ppermute(value, 'group', [(0, 1), (1, 0)])]
    ppermute x2, starting transfers between devices: 11.1 us -> 9.66 us  [swap_far(): lax.ppermute(value, 'tile', [(i, ((i + 1 ^ 1) - 1) % count) for i in rang...]
    ppermute x2, waiting for transfers between devices: 1.92 us -> 0.56 us  [swap_far(): lax.ppermute(value, 'tile', [(i, ((i + 1 ^ 1) - 1) % count) for i in rang...]
    ppermute x2, starting transfers between devices: 5.27 us -> 5.8 us  [swap_side(): return lax.ppermute(value, 'group', [(0, 1), (1, 0)])]
    pallas_call x2, Pallas kernels: 5.4 us -> 4.86 us  [the longest x1 2.74 us: per_device(): call(first_kernel, [tensor, tensor, pack, pack, pack, pack, pack], scratc...]
where the time goes in v1:
time: 28.8 us; the launch traced here: 28.6 us
  starting transfers between devices  15.6 us (54%)
  Pallas kernels  9.51 us (33%)
  waiting for transfers between devices  2.82 us (10%)
  between operations  0.67 us (2%)
    ppermute x2, starting transfers between devices, swap_far(): lax.ppermute(value, 'tile', [(i, ((i + 1 ^ 1) - 1) % count) for i in rang...  9.66 us
    ppermute x2, starting transfers between devices, swap_side(): return lax.ppermute(value, 'group', [(0, 1), (1, 0)])  5.8 us
    pallas_call x1, Pallas kernels, per_device(): call(last_kernel, [flat, messages], scratch, out_specs=in_hbm)  2.88 us
    pallas_call x1, Pallas kernels, per_device(): call(first_kernel, [tensor, tensor, pack, pack, pack, pack, pack], scratc...  2.74 us
    ppermute x2, waiting for transfers between devices, swap_side(): return lax.ppermute(value, 'group', [(0, 1), (1, 0)])  2.25 us
    pallas_call x1, Pallas kernels, per_device(): call(second_kernel, [packs] * 5)(a, at, edges, own, *exchange(*parts))  2.12 us
    pallas_call x1, Pallas kernels, per_device(): early = call(early_kernel, [tensor, spread, inner])(a, near, received[0])  1.77 us
  transfers between devices with their start and end apart: 6, of which 2 were waited for; matrix products, arithmetic and copies ran while one was open for 0% of the time, Pallas kernels for 6%

profile of v1, /device:TPU:0, one launch (start us, length us, event | category | flops | bytes accessed | tf_op | source)
XLA Modules:
  0.0 28.6 jit_solution(15511956145266585336)
XLA Ops:
  0.6 2.7 %shard_map.41 = (bf16[3,2,256,256]{3,2,1,0:T(8,128)(2,1)S(1)}, bf16[3,2,256,256]{3,2,1,0:T(8,128)(2,1)S(1)}, f32[16,128]{1,0:T(8,128)S(1)}, f32[16,128]{1,0:T(8,...) custom-call(bf16[3,1024,128]{2,1,0:T(8,128)(2,1)} %bitcast.12, f32[3,4,256]{2,1,0:T(4,128)} %bitcast.13), custom_call_target="tpu_custom_call" | custom-call | tf_op jit(solution)/shard_map/pallas_call | solution.py:438
  3.4 0.1 collective-permute-start
  3.5 7.4 %collective-permute-start.1 = (f32[16,128]{1,0:T(8,128)S(1)}, f32[16,128]{1,0:T(8,128)S(1)}, u32[]{:S(2)}, u32[]{:S(2)}) collective-permute-start(f32[16,128]{1,0:T(8,128)S(1)} %get-tuple-element.24), channel_id=1, source_target_pairs={{0,63},{1,2},{2,1},{3,4},{4,3},{5,6},{6,5},{7,8},{8,7},{9,10},{10,... | collective-permute-start | bytes 24584 | tf_op jit(solution)/shard_map/ppermute | solution.py:410
  10.9 2.9 %collective-permute-start.2 = (f32[16,128]{1,0:T(8,128)S(1)}, f32[16,128]{1,0:T(8,128)S(1)}, u32[]{:S(2)}, u32[]{:S(2)}) collective-permute-start(f32[16,128]{1,0:T(8,128)S(1)} %get-tuple-element.25), channel_id=1, source_target_pairs={{0,64},{64,0},{1,65},{65,1},{2,66},{66,2},{3,67},{67,3},{4,68},{68... | collective-permute-start | bytes 24584 | tf_op jit(solution)/shard_map/ppermute | solution.py:414
  13.8 0.0 collective-permute-done.near_in
  13.8 0.0 collective-permute-done.1.far_in
  13.8 2.2 %collective-permute-done.2.side_in = f32[16,128]{1,0:T(8,128)S(1)} collective-permute-done((f32[16,128]{1,0:T(8,128)S(1)}, f32[16,128]{1,0:T(8,128)S(1)}, u32[]{:S(2)}, u32[]{:S(2)}) %collective-permute-start.2) | collective-permute-done | bytes 8224 | tf_op jit(solution)/shard_map/ppermute | solution.py:414
  16.1 2.1 %shard_map.42 = (f32[32,128]{1,0:T(8,128)S(1)}, f32[32,128]{1,0:T(8,128)S(1)}, f32[32,128]{1,0:T(8,128)S(1)}, f32[32,128]{1,0:T(8,128)S(1)}, f32[32,128]{1,0:T(8,128)S(1)}) custom-call(bf16[3,2,256,256]{3,2,1,0:T(8,128)(2,1)S(1)} %get-tuple-element.19.a_ref, bf16[3,2,256,256]{3,2,1,0:T(8,128)(2,1)S(1)} %get-tuple-element.20.at_ref, ...), custom_call_target="tpu_custom_call" | custom-call | tf_op jit(solution)/shard_map/pallas_call | solution.py:441
  18.2 0.1 collective-permute-start.3
  18.3 2.2 %collective-permute-start.4 = (f32[32,128]{1,0:T(8,128)S(1)}, f32[32,128]{1,0:T(8,128)S(1)}, u32[]{:S(2)}, u32[]{:S(2)}) collective-permute-start(f32[32,128]{1,0:T(8,128)S(1)} %get-tuple-element.32), channel_id=1, source_target_pairs={{0,63},{1,2},{2,1},{3,4},{4,3},{5,6},{6,5},{7,8},{8,7},{9,10},{10,... | collective-permute-start | bytes 49160 | tf_op jit(solution)/shard_map/ppermute | solution.py:410
  20.5 2.9 %collective-permute-start.5 = (f32[32,128]{1,0:T(8,128)S(1)}, f32[32,128]{1,0:T(8,128)S(1)}, u32[]{:S(2)}, u32[]{:S(2)}) collective-permute-start(f32[32,128]{1,0:T(8,128)S(1)} %get-tuple-element.33), channel_id=1, source_target_pairs={{0,64},{64,0},{1,65},{65,1},{2,66},{66,2},{3,67},{67,3},{4,68},{68... | collective-permute-start | bytes 49160 | tf_op jit(solution)/shard_map/ppermute | solution.py:414
  23.4 0.0 collective-permute-done.3.near_in
  23.4 1.8 %shard_map.43 = (bf16[3,2,256,256]{3,2,1,0:T(8,128)(2,1)S(1)}, bf16[2,3,16,256]{3,2,1,0:T(8,128)(2,1)S(1)}, bf16[2,2,2,16,256]{4,3,2,1,0:T(8,128)(2,1)S(1)}) custom-call(bf16[3,2,256,256]{3,2,1,0:T(8,128)(2,1)S(1)} %get-tuple-element.19.a_ref, f32[32,128]{1,0:T(8,128)S(1)} %get-tuple-element.26.near_own, f32[32,128]{1,0:T(8,128)S(1)} %collective-permute-done.3.near_in), custom_call_target="tpu_custom_call" | custom-call | tf_op jit(solution)/shard_map/pallas_call | solution.py:445
  25.2 0.6 %collective-permute-done.4.far_in = f32[32,128]{1,0:T(8,128)S(1)} collective-permute-done((f32[32,128]{1,0:T(8,128)S(1)}, f32[32,128]{1,0:T(8,128)S(1)}, u32[]{:S(2)}, u32[]{:S(2)}) %collective-permute-start.4) | collective-permute-done | bytes 16416 | tf_op jit(solution)/shard_map/ppermute | solution.py:410
  25.7 0.0 collective-permute-done.5.side_in
  25.7 2.9 %shard_map.44 = (bf16[3,1024,128]{2,1,0:T(8,128)(2,1)}, f32[3,4,256]{2,1,0:T(4,128)}) custom-call(bf16[3,2,256,256]{3,2,1,0:T(8,128)(2,1)S(1)} %get-tuple-element.28.gated_ref, bf16[2,3,16,256]{3,2,1,0:T(8,128)(2,1)S(1)} %get-tuple-element.29.near_ref, bf16[2,2,2,16,256]{4,3,2,1,0:T(8,128)(2,1)S(1)} %get-tuple-element.30.inner_ref, ...), custom_call_target="tpu_custom_call" | custom-call | tf_op jit(solution)/shard_map/pallas_call | solution.py:446
Async XLA Ops:
  3.4 10.4 %collective-permute-start = (f32[16,128]{1,0:T(8,128)S(1)}, f32[16,128]{1,0:T(8,128)S(1)}, u32[]{:S(2)}, u32[]{:S(2)}) collective-permute-start(f32[16,128]{1,0:T(8,128)S(1)} %get-tuple-element.23), channel_id=1, source_target_pairs={{0,1},{1,0},{2,3},{3,2},{4,5},{5,4},{6,7},{7,6},{8,9},{9,8},{10,11... | collective-permute-start | bytes 24584 | tf_op jit(solution)/shard_map/ppermute | solution.py:405
  3.5 10.3 %collective-permute-start.1 = (f32[16,128]{1,0:T(8,128)S(1)}, f32[16,128]{1,0:T(8,128)S(1)}, u32[]{:S(2)}, u32[]{:S(2)}) collective-permute-start(f32[16,128]{1,0:T(8,128)S(1)} %get-tuple-element.24), channel_id=1, source_target_pairs={{0,63},{1,2},{2,1},{3,4},{4,3},{5,6},{6,5},{7,8},{8,7},{9,10},{10,... | collective-permute-start | bytes 24584 | tf_op jit(solution)/shard_map/ppermute | solution.py:410
  10.9 5.2 %collective-permute-start.2 = (f32[16,128]{1,0:T(8,128)S(1)}, f32[16,128]{1,0:T(8,128)S(1)}, u32[]{:S(2)}, u32[]{:S(2)}) collective-permute-start(f32[16,128]{1,0:T(8,128)S(1)} %get-tuple-element.25), channel_id=1, source_target_pairs={{0,64},{64,0},{1,65},{65,1},{2,66},{66,2},{3,67},{67,3},{4,68},{68... | collective-permute-start | bytes 24584 | tf_op jit(solution)/shard_map/ppermute | solution.py:414
  18.2 5.2 %collective-permute-start.3 = (f32[32,128]{1,0:T(8,128)S(1)}, f32[32,128]{1,0:T(8,128)S(1)}, u32[]{:S(2)}, u32[]{:S(2)}) collective-permute-start(f32[32,128]{1,0:T(8,128)S(1)} %get-tuple-element.27), channel_id=1, source_target_pairs={{0,1},{1,0},{2,3},{3,2},{4,5},{5,4},{6,7},{7,6},{8,9},{9,8},{10,11... | collective-permute-start | bytes 49160 | tf_op jit(solution)/shard_map/ppermute | solution.py:405
  18.3 7.5 %collective-permute-start.4 = (f32[32,128]{1,0:T(8,128)S(1)}, f32[32,128]{1,0:T(8,128)S(1)}, u32[]{:S(2)}, u32[]{:S(2)}) collective-permute-start(f32[32,128]{1,0:T(8,128)S(1)} %get-tuple-element.32), channel_id=1, source_target_pairs={{0,63},{1,2},{2,1},{3,4},{4,3},{5,6},{6,5},{7,8},{8,7},{9,10},{10,... | collective-permute-start | bytes 49160 | tf_op jit(solution)/shard_map/ppermute | solution.py:410
  20.5 5.2 %collective-permute-start.5 = (f32[32,128]{1,0:T(8,128)S(1)}, f32[32,128]{1,0:T(8,128)S(1)}, u32[]{:S(2)}, u32[]{:S(2)}) collective-permute-start(f32[32,128]{1,0:T(8,128)S(1)} %get-tuple-element.33), channel_id=1, source_target_pairs={{0,64},{64,0},{1,65},{65,1},{2,66},{66,2},{3,67},{67,3},{4,68},{68... | collective-permute-start | bytes 49160 | tf_op jit(solution)/shard_map/ppermute | solution.py:414

commit v2 on v1

--- a/solution.py
+++ b/solution.py
@@ -407,7 +407,14 @@
 
 def swap_far(value):
     count = lax.axis_size("tile")
-    return lax.ppermute(value, "tile", [(i, (((i + 1) ^ 1) - 1) % count) for i in range(count)])
+    pairs = []
+    for group in range(2):
+        for i in range(count):
+            other = ((i + 1) ^ 1) - 1
+            inner = 0 <= other < count
+            target = group * count + other if inner else (1 - group) * count + i
+            pairs.append((group * count + i, target))
+    return lax.ppermute(value, ("group", "tile"), pairs)
 
 
 def swap_side(value):

time: 28.8 us -> 25.6 us (0.89)
  the two profiles are of different devices: /device:TPU:0 before, /device:TPU:6 now
where the time goes in v2:
time: 25.6 us; the launch traced here: 25.4 us
  starting transfers between devices  12.4 us (48%)
  Pallas kernels  9.51 us (37%)
  waiting for transfers between devices  2.83 us (11%)
  between operations  0.67 us (3%)
    ppermute x2, starting transfers between devices, swap_far(): return lax.ppermute(value, ('group', 'tile'), pairs)  6.44 us
    ppermute x2, starting transfers between devices, swap_side(): return lax.ppermute(value, 'group', [(0, 1), (1, 0)])  5.79 us
    pallas_call x1, Pallas kernels, per_device(): call(last_kernel, [flat, messages], scratch, out_specs=in_hbm)  2.88 us
    pallas_call x1, Pallas kernels, per_device(): call(first_kernel, [tensor, tensor, pack, pack, pack, pack, pack], scratc...  2.74 us
    ppermute x2, waiting for transfers between devices, swap_side(): return lax.ppermute(value, 'group', [(0, 1), (1, 0)])  2.26 us
    pallas_call x1, Pallas kernels, per_device(): call(second_kernel, [packs] * 5)(a, at, edges, own, *exchange(*parts))  2.12 us
    pallas_call x1, Pallas kernels, per_device(): early = call(early_kernel, [tensor, spread, inner])(a, near, received[0])  1.77 us
    ppermute x2, waiting for transfers between devices, swap_far(): return lax.ppermute(value, ('group', 'tile'), pairs)  0.56 us
  transfers between devices with their start and end apart: 6, of which 2 were waited for; matrix products, arithmetic and copies ran while one was open for 0% of the time, Pallas kernels for 7%

profile of v2, /device:TPU:6, one launch (start us, length us, event | category | flops | bytes accessed | tf_op | source)
XLA Modules:
  0.0 25.4 jit_solution(9929720303827064559)
XLA Ops:
  0.6 2.7 %shard_map.41 = (bf16[3,2,256,256]{3,2,1,0:T(8,128)(2,1)S(1)}, bf16[3,2,256,256]{3,2,1,0:T(8,128)(2,1)S(1)}, f32[16,128]{1,0:T(8,128)S(1)}, f32[16,128]{1,0:T(8,...) custom-call(bf16[3,1024,128]{2,1,0:T(8,128)(2,1)} %bitcast.12, f32[3,4,256]{2,1,0:T(4,128)} %bitcast.13), custom_call_target="tpu_custom_call" | custom-call | tf_op jit(solution)/shard_map/pallas_call | solution.py:445
  3.4 0.1 collective-permute-start
  3.5 5.4 %collective-permute-start.1 = (f32[16,128]{1,0:T(8,128)S(1)}, f32[16,128]{1,0:T(8,128)S(1)}, u32[]{:S(2)}, u32[]{:S(2)}) collective-permute-start(f32[16,128]{1,0:T(8,128)S(1)} %get-tuple-element.24), channel_id=1, source_target_pairs={{0,64},{1,2},{2,1},{3,4},{4,3},{5,6},{6,5},{7,8},{8,7},{9,10},{10,... | collective-permute-start | bytes 24584 | tf_op jit(solution)/shard_map/ppermute | solution.py:417
  8.9 2.9 %collective-permute-start.2 = (f32[16,128]{1,0:T(8,128)S(1)}, f32[16,128]{1,0:T(8,128)S(1)}, u32[]{:S(2)}, u32[]{:S(2)}) collective-permute-start(f32[16,128]{1,0:T(8,128)S(1)} %get-tuple-element.25), channel_id=1, source_target_pairs={{0,64},{64,0},{1,65},{65,1},{2,66},{66,2},{3,67},{67,3},{4,68},{68... | collective-permute-start | bytes 24584 | tf_op jit(solution)/shard_map/ppermute | solution.py:421
  11.8 0.0 collective-permute-done.near_in
  11.8 0.0 collective-permute-done.1.far_in
  11.8 2.2 %collective-permute-done.2.side_in = f32[16,128]{1,0:T(8,128)S(1)} collective-permute-done((f32[16,128]{1,0:T(8,128)S(1)}, f32[16,128]{1,0:T(8,128)S(1)}, u32[]{:S(2)}, u32[]{:S(2)}) %collective-permute-start.2) | collective-permute-done | bytes 8224 | tf_op jit(solution)/shard_map/ppermute | solution.py:421
  14.0 2.1 %shard_map.42 = (f32[32,128]{1,0:T(8,128)S(1)}, f32[32,128]{1,0:T(8,128)S(1)}, f32[32,128]{1,0:T(8,128)S(1)}, f32[32,128]{1,0:T(8,128)S(1)}, f32[32,128]{1,0:T(8,128)S(1)}) custom-call(bf16[3,2,256,256]{3,2,1,0:T(8,128)(2,1)S(1)} %get-tuple-element.19.a_ref, bf16[3,2,256,256]{3,2,1,0:T(8,128)(2,1)S(1)} %get-tuple-element.20.at_ref, ...), custom_call_target="tpu_custom_call" | custom-call | tf_op jit(solution)/shard_map/pallas_call | solution.py:448
  16.2 0.1 collective-permute-start.3
  16.3 1.0 %collective-permute-start.4 = (f32[32,128]{1,0:T(8,128)S(1)}, f32[32,128]{1,0:T(8,128)S(1)}, u32[]{:S(2)}, u32[]{:S(2)}) collective-permute-start(f32[32,128]{1,0:T(8,128)S(1)} %get-tuple-element.32), channel_id=1, source_target_pairs={{0,64},{1,2},{2,1},{3,4},{4,3},{5,6},{6,5},{7,8},{8,7},{9,10},{10,... | collective-permute-start | bytes 49160 | tf_op jit(solution)/shard_map/ppermute | solution.py:417
  17.3 2.9 %collective-permute-start.5 = (f32[32,128]{1,0:T(8,128)S(1)}, f32[32,128]{1,0:T(8,128)S(1)}, u32[]{:S(2)}, u32[]{:S(2)}) collective-permute-start(f32[32,128]{1,0:T(8,128)S(1)} %get-tuple-element.33), channel_id=1, source_target_pairs={{0,64},{64,0},{1,65},{65,1},{2,66},{66,2},{3,67},{67,3},{4,68},{68... | collective-permute-start | bytes 49160 | tf_op jit(solution)/shard_map/ppermute | solution.py:421
  20.2 0.0 collective-permute-done.3.near_in
  20.2 1.8 %shard_map.43 = (bf16[3,2,256,256]{3,2,1,0:T(8,128)(2,1)S(1)}, bf16[2,3,16,256]{3,2,1,0:T(8,128)(2,1)S(1)}, bf16[2,2,2,16,256]{4,3,2,1,0:T(8,128)(2,1)S(1)}) custom-call(bf16[3,2,256,256]{3,2,1,0:T(8,128)(2,1)S(1)} %get-tuple-element.19.a_ref, f32[32,128]{1,0:T(8,128)S(1)} %get-tuple-element.26.near_own, f32[32,128]{1,0:T(8,128)S(1)} %collective-permute-done.3.near_in), custom_call_target="tpu_custom_call" | custom-call | tf_op jit(solution)/shard_map/pallas_call | solution.py:452
  22.0 0.6 %collective-permute-done.4.far_in = f32[32,128]{1,0:T(8,128)S(1)} collective-permute-done((f32[32,128]{1,0:T(8,128)S(1)}, f32[32,128]{1,0:T(8,128)S(1)}, u32[]{:S(2)}, u32[]{:S(2)}) %collective-permute-start.4) | collective-permute-done | bytes 16416 | tf_op jit(solution)/shard_map/ppermute | solution.py:417
  22.5 0.0 collective-permute-done.5.side_in
  22.5 2.9 %shard_map.44 = (bf16[3,1024,128]{2,1,0:T(8,128)(2,1)}, f32[3,4,256]{2,1,0:T(4,128)}) custom-call(bf16[3,2,256,256]{3,2,1,0:T(8,128)(2,1)S(1)} %get-tuple-element.28.gated_ref, bf16[2,3,16,256]{3,2,1,0:T(8,128)(2,1)S(1)} %get-tuple-element.29.near_ref, bf16[2,2,2,16,256]{4,3,2,1,0:T(8,128)(2,1)S(1)} %get-tuple-element.30.inner_ref, ...), custom_call_target="tpu_custom_call" | custom-call | tf_op jit(solution)/shard_map/pallas_call | solution.py:453
Async XLA Ops:
  3.4 8.4 %collective-permute-start = (f32[16,128]{1,0:T(8,128)S(1)}, f32[16,128]{1,0:T(8,128)S(1)}, u32[]{:S(2)}, u32[]{:S(2)}) collective-permute-start(f32[16,128]{1,0:T(8,128)S(1)} %get-tuple-element.23), channel_id=1, source_target_pairs={{0,1},{1,0},{2,3},{3,2},{4,5},{5,4},{6,7},{7,6},{8,9},{9,8},{10,11... | collective-permute-start | bytes 24584 | tf_op jit(solution)/shard_map/ppermute | solution.py:405
  3.5 8.3 %collective-permute-start.1 = (f32[16,128]{1,0:T(8,128)S(1)}, f32[16,128]{1,0:T(8,128)S(1)}, u32[]{:S(2)}, u32[]{:S(2)}) collective-permute-start(f32[16,128]{1,0:T(8,128)S(1)} %get-tuple-element.24), channel_id=1, source_target_pairs={{0,64},{1,2},{2,1},{3,4},{4,3},{5,6},{6,5},{7,8},{8,7},{9,10},{10,... | collective-permute-start | bytes 24584 | tf_op jit(solution)/shard_map/ppermute | solution.py:417
  8.9 5.2 %collective-permute-start.2 = (f32[16,128]{1,0:T(8,128)S(1)}, f32[16,128]{1,0:T(8,128)S(1)}, u32[]{:S(2)}, u32[]{:S(2)}) collective-permute-start(f32[16,128]{1,0:T(8,128)S(1)} %get-tuple-element.25), channel_id=1, source_target_pairs={{0,64},{64,0},{1,65},{65,1},{2,66},{66,2},{3,67},{67,3},{4,68},{68... | collective-permute-start | bytes 24584 | tf_op jit(solution)/shard_map/ppermute | solution.py:421
  16.2 4.0 %collective-permute-start.3 = (f32[32,128]{1,0:T(8,128)S(1)}, f32[32,128]{1,0:T(8,128)S(1)}, u32[]{:S(2)}, u32[]{:S(2)}) collective-permute-start(f32[32,128]{1,0:T(8,128)S(1)} %get-tuple-element.27), channel_id=1, source_target_pairs={{0,1},{1,0},{2,3},{3,2},{4,5},{5,4},{6,7},{7,6},{8,9},{9,8},{10,11... | collective-permute-start | bytes 49160 | tf_op jit(solution)/shard_map/ppermute | solution.py:405
  16.3 6.3 %collective-permute-start.4 = (f32[32,128]{1,0:T(8,128)S(1)}, f32[32,128]{1,0:T(8,128)S(1)}, u32[]{:S(2)}, u32[]{:S(2)}) collective-permute-start(f32[32,128]{1,0:T(8,128)S(1)} %get-tuple-element.32), channel_id=1, source_target_pairs={{0,64},{1,2},{2,1},{3,4},{4,3},{5,6},{6,5},{7,8},{8,7},{9,10},{10,... | collective-permute-start | bytes 49160 | tf_op jit(solution)/shard_map/ppermute | solution.py:417
  17.3 5.2 %collective-permute-start.5 = (f32[32,128]{1,0:T(8,128)S(1)}, f32[32,128]{1,0:T(8,128)S(1)}, u32[]{:S(2)}, u32[]{:S(2)}) collective-permute-start(f32[32,128]{1,0:T(8,128)S(1)} %get-tuple-element.33), channel_id=1, source_target_pairs={{0,64},{64,0},{1,65},{65,1},{2,66},{66,2},{3,67},{67,3},{4,68},{68... | collective-permute-start | bytes 49160 | tf_op jit(solution)/shard_map/ppermute | solution.py:421

commit v3 on v2

--- a/solution.py
+++ b/solution.py
@@ -60,7 +60,7 @@
 
 
 def kron(rep, tile):
-    return (rep.astype(f32)[:, None, :] * tile.astype(f32)[None, :, :]).astype(bf16).reshape(SQ, SQ)
+    return (rep.astype(bf16)[:, None, :] * tile.astype(bf16)[None, :, :]).reshape(SQ, SQ)
 
 
 def place():
@@ -81,12 +81,10 @@
     return pack
 
 
-def packs_of(blocks):
-    first_half, even, _ = place()
-    near = [jnp.where(even, blocks[DOWN][i], blocks[UP][i]) for i in range(SITES)]
-    far = [jnp.where(even, blocks[UP][i], blocks[DOWN][i]) for i in range(SITES)]
-    side = jnp.where(first_half, blocks[RIGHT][2], blocks[LEFT][0])
-    inner = [blocks[RIGHT][0], blocks[RIGHT][1], blocks[LEFT][1], blocks[LEFT][2]]
+def packs_of(near, far, left, right):
+    first_half, _, _ = place()
+    side = jnp.where(first_half, right[2], left[0])
+    inner = [right[0], right[1], left[1], left[2]]
     return pack_of(near + inner), pack_of(far + [side])
 
 
@@ -106,21 +104,29 @@
     return jnp.concatenate([part, part], axis=1)
 
 
-def site_parts(a_ref, at_ref, site, up, left, down, right, split_states):
-    parts = {leg: [] for leg in LEGS}
-    for first, second, m_rep, m_tile, k_rep, k_tile, leg_rep, leg_tile in (
-        (a_ref, at_ref, up, left, down, right, UP, LEFT),
-        (at_ref, a_ref, down, right, up, left, DOWN, RIGHT),
+def product(x_ref, form, site, s, weight):
+    kept = dot(x_ref[form, site, s], weight).astype(bf16)
+    return dot(kept, x_ref[1 - form, site, s])
+
+
+def fold_minor(full, form):
+    return jnp.sum(full.reshape(D, D, SQ) * form[None, :, :], axis=1)
+
+
+def fold_major(full, form):
+    return jnp.sum(full.reshape(D, D, SQ) * form[:, None, :], axis=0)
+
+
+def site_parts(x_ref, site, up, left, down, right):
+    parts = {}
+    for form, m_rep, m_tile, k_rep, k_tile, leg_rep, leg_tile in (
+        (0, up, left, down, right, UP, LEFT),
+        (1, down, right, up, left, DOWN, RIGHT),
     ):
         weight = kron(k_rep, k_tile)
-        kept = [dot(first[site, s], weight).astype(bf16) for s in range(STATES)]
-        products = [dot(kept[s], second[site, s]) for s in range(STATES)]
-        if not split_states:
-            products = [products[0] + products[1]]
-        for product in products:
-            cube = product.reshape(D, D, SQ)
-            parts[leg_rep].append(jnp.sum(cube * m_tile[None, :, :], axis=1))
-            parts[leg_tile].append(jnp.sum(cube * m_rep[:, None, :], axis=0))
+        full = product(x_ref, form, site, 0, weight) + product(x_ref, form, site, 1, weight)
+        parts[leg_rep] = [fold_minor(full, m_tile)]
+        parts[leg_tile] = [fold_major(full, m_rep)]
     return parts
 
 
@@ -132,7 +138,7 @@
         ((LEFT, RIGHT), selector(minor, minor, WIDE)),
     ):
         rows = [parts[site][leg][s] for leg in legs for site in range(SITES) for s in range(count)]
-        blocks = dot_split(jnp.concatenate(rows, axis=0), pick).reshape(2, SITES, count, D, WIDE)
+        blocks = dot(jnp.concatenate(rows, axis=0).astype(bf16), pick).reshape(2, SITES, count, D, WIDE)
         for index, leg in enumerate(legs):
             block = blocks[index]
             summed = block[:, 0] + block[:, 1] if split_states else block[:, 0]
@@ -149,7 +155,7 @@
 
 
 def first_kernel(
-    x_ref, msg_ref, a_ref, at_ref, edge_ref, own_ref, near_ref, far_ref, side_ref,
+    x_ref, msg_ref, form_ref, edge_ref, own_ref, near_ref, far_ref, side_ref,
     x_buf, msg_buf, wide_ref, sems,
 ):
     copies = [
@@ -183,16 +189,15 @@
         for s in range(STATES):
             halves = [wide_ref[site, pl.ds(2 * half + s, SQ, stride=4), :] for half in range(2)]
             block = jnp.concatenate(halves, axis=1)
-            a_ref[site, s] = block.astype(bf16)
-            at_ref[site, s] = block.T.astype(bf16)
+            form_ref[0, site, s] = block.astype(bf16)
+            form_ref[1, site, s] = block.T.astype(bf16)
         parts.append(
-            site_parts(
-                a_ref, at_ref, site,
-                ends[0, site], sides[0, site], ends[1, site], sides[1, site], False,
-            )
+            site_parts(form_ref, site, ends[0, site], sides[0, site], ends[1, site], sides[1, site])
         )
     out, _ = finish(parts, False)
-    near, far = packs_of(out)
+    near = [jnp.where(even, out[DOWN][i], out[UP][i]) for i in range(SITES)]
+    far = [jnp.where(even, out[UP][i], out[DOWN][i]) for i in range(SITES)]
+    near, far = packs_of(near, far, out[LEFT], out[RIGHT])
     own_ref[...] = near
     near_ref[...] = near
     far_ref[...] = far
@@ -214,22 +219,91 @@
     }
 
 
+def site_forms(near, edge, own, far=None, side=None):
+    first_half, even, _ = place()
+
+    def pick(one, two):
+        return jnp.where(first_half, one, two)
+
+    sites = [1, pick(0, 2), pick(2, 0)]
+    outer, near_side = tile(edge, 3), None if side is None else tile(side, 3)
+    sides = [
+        (tile(own, 3), tile(own, 6)),
+        (pick(outer, tile(own, 4)), pick(tile(own, 5), outer)),
+    ]
+    if side is not None:
+        sides.append((pick(tile(own, 4), near_side), pick(near_side, tile(own, 5))))
+    forms = []
+    for index, (left, right) in enumerate(sides):
+        ends = []
+        for pack in (near, far):
+            if pack is None:
+                ends.append(None)
+            elif index == 0:
+                ends.append(rep(pack, 1))
+            else:
+                zero, two = rep(pack, 0), rep(pack, 2)
+                ends.append(pick(zero, two) if index == 1 else pick(two, zero))
+        forms.append((sites[index], *ends, jnp.where(even, right, left), jnp.where(even, left, right)))
+    return forms
+
+
+def rounded(ref):
+    return ref[...].astype(bf16).astype(f32)
+
+
+def parity():
+    return lax.axis_index("tile") & 1
+
+
+def ahead_kernel(form_ref, edge_ref, near_own, near_in, full_ref, part_ref):
+    form = parity()
+    forms = site_forms(rounded(near_in), rounded(edge_ref), rounded(near_own))
+    for index, (site, near, _, with_near, with_far) in enumerate(forms):
+        weight = kron(near, with_near)
+        for s in range(STATES):
+            full = product(form_ref, form, site, s, weight)
+            full_ref[index, s] = full
+            part_ref[index, s] = fold_minor(full, with_far)
+
+
 def second_kernel(
-    a_ref, at_ref, edge_ref, near_own, near_in, far_in, side_in,
+    form_ref, edge_ref, near_own, near_in, far_in, side_in, full_ref, part_ref,
     own_near_ref, own_far_ref, near_ref, far_ref, side_ref,
 ):
-    def rounded(ref):
-        return ref[...].astype(bf16).astype(f32)
-
-    where = incoming_packs(*(rounded(ref) for ref in (near_own, edge_ref, near_in, far_in, side_in)))
+    first_half, even, at_end = place()
+    form = parity()
+    edge = rounded(edge_ref)
+    far = jnp.where(at_end, edge, rounded(far_in))
+    forms = site_forms(rounded(near_in), edge, rounded(near_own), far, rounded(side_in))
     parts = []
-    for site in range(SITES):
-        forms = [
-            (rep if leg in (UP, DOWN) else tile)(*where[leg][site]) for leg in range(4)
-        ]
-        parts.append(site_parts(a_ref, at_ref, site, *forms, True))
+    for index, (site, near, far, with_near, with_far) in enumerate(forms):
+        legs = {leg: [] for leg in LEGS}
+        ahead, behind = kron(near, with_near), kron(far, with_far)
+        for s in range(STATES):
+            if index < 2:
+                full, part = full_ref[index, s], part_ref[index, s]
+            else:
+                full = product(form_ref, form, site, s, ahead)
+                part = fold_minor(full, with_far)
+            legs[UP].append(part)
+            legs[LEFT].append(fold_major(full, far))
+            full = product(form_ref, 1 - form, site, s, behind)
+            legs[DOWN].append(fold_minor(full, with_near))
+            legs[RIGHT].append(fold_major(full, near))
+        parts.append(legs)
+
+    def by_site(values):
+        middle, outer, inner = values
+        return [jnp.where(first_half, outer, inner), middle, jnp.where(first_half, inner, outer)]
+
     for index, values in enumerate(finish(parts, True)):
-        near, far = packs_of(values)
+        near, far, with_far, with_near = (
+            by_site([values[leg][i] for i in range(SITES)]) for leg in (DOWN, UP, LEFT, RIGHT)
+        )
+        left = [jnp.where(even, with_far[i], with_near[i]) for i in range(SITES)]
+        right = [jnp.where(even, with_near[i], with_far[i]) for i in range(SITES)]
+        near, far = packs_of(near, far, left, right)
         part = slice(index * D, index * D + D)
         own_near_ref[part] = near
         own_far_ref[part] = far
@@ -307,7 +381,7 @@
     return results
 
 
-def early_kernel(a_ref, near_own, near_in, gated_ref, near_ref, inner_ref):
+def early_kernel(form_ref, near_own, near_in, gated_ref, near_ref, inner_ref):
     _, even, _ = place()
     slots = slot_of_lane()
     other = (iota((D, WIDE), 1) + 2 * D) & (WIDE - 1)
@@ -319,7 +393,7 @@
         both.append(jnp.where(slots < 5, own + mate, 0.0))
     grow, mix = math.cosh(field_step), math.sinh(field_step)
     for site in range(SITES):
-        tensors = [a_ref[site, s].astype(f32) for s in range(STATES)]
+        tensors = [form_ref[0, site, s].astype(f32) for s in range(STATES)]
         for s in range(STATES):
             gated_ref[site, s] = (grow * tensors[s] + mix * tensors[1 - s]).astype(bf16)
     plain, flipped = bond_weights(*both, slots < 0)
@@ -338,6 +412,16 @@
 ):
     first_half, even, at_end = place()
     slots = slot_of_lane()
+    where = incoming_packs(
+        near_own[:D], edge_ref[...], near_in[:D], far_in[:D], side_in[:D]
+    )
+    own_row = iota((D, SQ), 0) == major(iota((D, SQ), 1))
+    for leg in LEGS:
+        for site in range(SITES):
+            spread = jnp.where(own_row, tile(*where[leg][site]), 0.0)
+            msg_buf[site, leg : leg + 1] = jnp.sum(spread, axis=0, keepdims=True)
+    msg_copy = pltpu.make_async_copy(msg_buf, messages_ref, sems.at[SITES])
+    msg_copy.start()
     both = []
     for index in range(2):
         part = slice(index * D, index * D + D)
@@ -356,16 +440,6 @@
         lefts = [jnp.where(first_half, identity, side), inner_ref[s, 1, 0], inner_ref[s, 1, 1]]
         rights = [inner_ref[s, 0, 0], inner_ref[s, 0, 1], jnp.where(first_half, side, identity)]
         factors.append((ups, downs, lefts, rights))
-    where = incoming_packs(
-        near_own[:D], edge_ref[...], near_in[:D], far_in[:D], side_in[:D]
-    )
-    own_row = iota((D, SQ), 0) == major(iota((D, SQ), 1))
-    for leg in LEGS:
-        for site in range(SITES):
-            spread = jnp.where(own_row, tile(*where[leg][site]), 0.0)
-            msg_buf[site, leg : leg + 1] = jnp.sum(spread, axis=0, keepdims=True)
-    msg_copy = pltpu.make_async_copy(msg_buf, messages_ref, sems.at[SITES])
-    msg_copy.start()
     copies = []
     for site in range(SITES):
         for s in range(STATES):
@@ -442,14 +516,18 @@
         pltpu.VMEM((SITES, 4 * SQ, 128), f32),
         pltpu.SemaphoreType.DMA((SITES + 1,)),
     ]
-    a, at, edges, own, *parts = call(
-        first_kernel, [tensor, tensor, pack, pack, pack, pack, pack], scratch, in_specs=in_hbm
+    forms, edges, own, *parts = call(
+        first_kernel, [((2, *tensor[0]), bf16), pack, pack, pack, pack, pack], scratch, in_specs=in_hbm
     )(x, msg)
-    near, far, *parts = call(second_kernel, [packs] * 5)(a, at, edges, own, *exchange(*parts))
+    received = exchange(*parts)
+    ahead = call(
+        ahead_kernel, [((2, STATES, SQ, SQ), f32), ((2, STATES, D, SQ), f32)]
+    )(forms, edges, own, received[0])
+    near, far, *parts = call(second_kernel, [packs] * 5)(forms, edges, own, *received, *ahead)
     received = exchange(*parts)
     spread = ((STATES, SITES, D, SQ), bf16)
     inner = ((STATES, 2, 2, D, SQ), bf16)
-    early = call(early_kernel, [tensor, spread, inner])(a, near, received[0])
+    early = call(early_kernel, [tensor, spread, inner])(forms, near, received[0])
     x, messages = call(last_kernel, [flat, messages], scratch, out_specs=in_hbm)(
         *early, edges, near, far, *received
     )

time: 25.6 us -> 24.6 us (0.961)
  waiting for transfers between devices: 2.83 us -> 2.17 us
  Pallas kernels: 9.51 us -> 9.21 us
    ppermute x2, waiting for transfers between devices: 2.26 us -> 1.6 us  [swap_side(): return lax.ppermute(value, 'group', [(0, 1), (1, 0)])]
    pallas_call x3 -> x4, Pallas kernels: 6.63 us -> 6.34 us  [the longest x1 2.71 us: per_device(): call(first_kernel, [((2, *tensor[0]), bf16), pack, pack, pack, pack, pack...]
  transfers between devices with their start and end apart: 6 -> 6, of which waited for: 2 -> 2; matrix products, arithmetic and copies ran while one was open for 0% -> 0% of each run, Pallas kernels for 7% -> 10%
where the time goes in v3:
time: 24.6 us; the launch traced here: 24.5 us
  starting transfers between devices  12.4 us (50%)
  Pallas kernels  9.21 us (37%)
  waiting for transfers between devices  2.17 us (9%)
  between operations  0.69 us (3%)
    ppermute x2, starting transfers between devices, swap_far(): return lax.ppermute(value, ('group', 'tile'), pairs)  6.43 us
    ppermute x2, starting transfers between devices, swap_side(): return lax.ppermute(value, 'group', [(0, 1), (1, 0)])  5.8 us
    pallas_call x1, Pallas kernels, per_device(): call(last_kernel, [flat, messages], scratch, out_specs=in_hbm)  2.86 us
    pallas_call x1, Pallas kernels, per_device(): call(first_kernel, [((2, *tensor[0]), bf16), pack, pack, pack, pack, pack...  2.71 us
    pallas_call x1, Pallas kernels, per_device(): call(early_kernel, [tensor, spread, inner])(forms, near, received[0])  1.77 us
    ppermute x2, waiting for transfers between devices, swap_side(): return lax.ppermute(value, 'group', [(0, 1), (1, 0)])  1.6 us
    pallas_call x1, Pallas kernels, per_device(): call(second_kernel, [packs] * 5)(forms, edges, own, *received, *ahead)  1.23 us
    pallas_call x1, Pallas kernels, per_device(): call(ahead_kernel, [((2, STATES, SQ, SQ), f32), ((2, STATES, D, SQ), f32)])  0.63 us
  transfers between devices with their start and end apart: 6, of which 2 were waited for; matrix products, arithmetic and copies ran while one was open for 0% of the time, Pallas kernels for 10%

profile of v3, /device:TPU:6, one launch (start us, length us, event | category | flops | bytes accessed | tf_op | source)
XLA Modules:
  0.0 24.5 jit_solution(16003725534191249217)
XLA Ops:
  0.6 2.7 %shard_map.41 = (bf16[2,3,2,256,256]{4,3,2,1,0:T(8,128)(2,1)S(1)}, f32[16,128]{1,0:T(8,128)S(1)}, f32[16,128]{1,0:T(8,128)S(1)}, f32[16,128]{1,0:T(8,128)S(1)}, ...) custom-call(bf16[3,1024,128]{2,1,0:T(8,128)(2,1)} %bitcast.12, f32[3,4,256]{2,1,0:T(4,128)} %bitcast.13), custom_call_target="tpu_custom_call" | custom-call | tf_op jit(solution)/shard_map/pallas_call | solution.py:519
  3.3 0.1 collective-permute-start
  3.4 5.4 %collective-permute-start.1 = (f32[16,128]{1,0:T(8,128)S(1)}, f32[16,128]{1,0:T(8,128)S(1)}, u32[]{:S(2)}, u32[]{:S(2)}) collective-permute-start(f32[16,128]{1,0:T(8,128)S(1)} %get-tuple-element.24), channel_id=1, source_target_pairs={{0,64},{1,2},{2,1},{3,4},{4,3},{5,6},{6,5},{7,8},{8,7},{9,10},{10,... | collective-permute-start | bytes 24584 | tf_op jit(solution)/shard_map/ppermute | solution.py:491
  8.9 2.9 %collective-permute-start.2 = (f32[16,128]{1,0:T(8,128)S(1)}, f32[16,128]{1,0:T(8,128)S(1)}, u32[]{:S(2)}, u32[]{:S(2)}) collective-permute-start(f32[16,128]{1,0:T(8,128)S(1)} %get-tuple-element.25), channel_id=1, source_target_pairs={{0,64},{64,0},{1,65},{65,1},{2,66},{66,2},{3,67},{67,3},{4,68},{68... | collective-permute-start | bytes 24584 | tf_op jit(solution)/shard_map/ppermute | solution.py:495
  11.8 0.0 collective-permute-done.near_in
  11.8 0.6 %shard_map.42 = (f32[2,2,256,256]{3,2,1,0:T(8,128)S(1)}, f32[2,2,16,256]{3,2,1,0:T(8,128)S(1)}) custom-call(bf16[2,3,2,256,256]{4,3,2,1,0:T(8,128)(2,1)S(1)} %get-tuple-element.20.form_ref, f32[16,128]{1,0:T(8,128)S(1)} %get-tuple-element.21.edge_ref, f32[16,128]{1,0:T(8,128)S(1)} %get-tuple-element.22.near_own, f32[16,128]{1,0:T(8,128)S(1)} %collective-permute-done.near_in), custom_call_target="tpu_custom_call" | custom-call | tf_op jit(solution)/shard_map/pallas_call | solution.py:523
  12.4 0.0 collective-permute-done.1.far_in
  12.4 1.6 %collective-permute-done.2.side_in = f32[16,128]{1,0:T(8,128)S(1)} collective-permute-done((f32[16,128]{1,0:T(8,128)S(1)}, f32[16,128]{1,0:T(8,128)S(1)}, u32[]{:S(2)}, u32[]{:S(2)}) %collective-permute-start.2) | collective-permute-done | bytes 8224 | tf_op jit(solution)/shard_map/ppermute | solution.py:495
  14.0 1.2 %shard_map.43 = (f32[32,128]{1,0:T(8,128)S(1)}, f32[32,128]{1,0:T(8,128)S(1)}, f32[32,128]{1,0:T(8,128)S(1)}, f32[32,128]{1,0:T(8,128)S(1)}, f32[32,128]{1,0:T(8,128)S(1)}) custom-call(bf16[2,3,2,256,256]{4,3,2,1,0:T(8,128)(2,1)S(1)} %get-tuple-element.20.form_ref, f32[16,128]{1,0:T(8,128)S(1)} %get-tuple-element.21.edge_ref, ...), custom_call_target="tpu_custom_call" | custom-call | tf_op jit(solution)/shard_map/pallas_call | solution.py:526
  15.3 0.1 collective-permute-start.3
  15.3 1.0 %collective-permute-start.4 = (f32[32,128]{1,0:T(8,128)S(1)}, f32[32,128]{1,0:T(8,128)S(1)}, u32[]{:S(2)}, u32[]{:S(2)}) collective-permute-start(f32[32,128]{1,0:T(8,128)S(1)} %get-tuple-element.34), channel_id=1, source_target_pairs={{0,64},{1,2},{2,1},{3,4},{4,3},{5,6},{6,5},{7,8},{8,7},{9,10},{10,... | collective-permute-start | bytes 49160 | tf_op jit(solution)/shard_map/ppermute | solution.py:491
  16.4 2.9 %collective-permute-start.5 = (f32[32,128]{1,0:T(8,128)S(1)}, f32[32,128]{1,0:T(8,128)S(1)}, u32[]{:S(2)}, u32[]{:S(2)}) collective-permute-start(f32[32,128]{1,0:T(8,128)S(1)} %get-tuple-element.35), channel_id=1, source_target_pairs={{0,64},{64,0},{1,65},{65,1},{2,66},{66,2},{3,67},{67,3},{4,68},{68... | collective-permute-start | bytes 49160 | tf_op jit(solution)/shard_map/ppermute | solution.py:495
  19.3 0.0 collective-permute-done.3.near_in
  19.3 1.8 %shard_map.44 = (bf16[3,2,256,256]{3,2,1,0:T(8,128)(2,1)S(1)}, bf16[2,3,16,256]{3,2,1,0:T(8,128)(2,1)S(1)}, bf16[2,2,2,16,256]{4,3,2,1,0:T(8,128)(2,1)S(1)}) custom-call(bf16[2,3,2,256,256]{4,3,2,1,0:T(8,128)(2,1)S(1)} %get-tuple-element.20.form_ref, f32[32,128]{1,0:T(8,128)S(1)} %get-tuple-element.28.near_own, f32[32,128]{1,0:T(8,128)S(1)} %collective-permute-done.3.near_in), custom_call_target="tpu_custom_call" | custom-call | tf_op jit(solution)/shard_map/pallas_call | solution.py:530
  21.0 0.6 %collective-permute-done.4.far_in = f32[32,128]{1,0:T(8,128)S(1)} collective-permute-done((f32[32,128]{1,0:T(8,128)S(1)}, f32[32,128]{1,0:T(8,128)S(1)}, u32[]{:S(2)}, u32[]{:S(2)}) %collective-permute-start.4) | collective-permute-done | bytes 16416 | tf_op jit(solution)/shard_map/ppermute | solution.py:491
  21.6 0.0 collective-permute-done.5.side_in
  21.6 2.9 %shard_map.45 = (bf16[3,1024,128]{2,1,0:T(8,128)(2,1)}, f32[3,4,256]{2,1,0:T(4,128)}) custom-call(bf16[3,2,256,256]{3,2,1,0:T(8,128)(2,1)S(1)} %get-tuple-element.30.gated_ref, bf16[2,3,16,256]{3,2,1,0:T(8,128)(2,1)S(1)} %get-tuple-element.31.near_ref, bf16[2,2,2,16,256]{4,3,2,1,0:T(8,128)(2,1)S(1)} %get-tuple-element.32.inner_ref, ...), custom_call_target="tpu_custom_call" | custom-call | tf_op jit(solution)/shard_map/pallas_call | solution.py:531
Async XLA Ops:
  3.3 8.4 %collective-permute-start = (f32[16,128]{1,0:T(8,128)S(1)}, f32[16,128]{1,0:T(8,128)S(1)}, u32[]{:S(2)}, u32[]{:S(2)}) collective-permute-start(f32[16,128]{1,0:T(8,128)S(1)} %get-tuple-element.23), channel_id=1, source_target_pairs={{0,1},{1,0},{2,3},{3,2},{4,5},{5,4},{6,7},{7,6},{8,9},{9,8},{10,11... | collective-permute-start | bytes 24584 | tf_op jit(solution)/shard_map/ppermute | solution.py:479
  3.4 9.0 %collective-permute-start.1 = (f32[16,128]{1,0:T(8,128)S(1)}, f32[16,128]{1,0:T(8,128)S(1)}, u32[]{:S(2)}, u32[]{:S(2)}) collective-permute-start(f32[16,128]{1,0:T(8,128)S(1)} %get-tuple-element.24), channel_id=1, source_target_pairs={{0,64},{1,2},{2,1},{3,4},{4,3},{5,6},{6,5},{7,8},{8,7},{9,10},{10,... | collective-permute-start | bytes 24584 | tf_op jit(solution)/shard_map/ppermute | solution.py:491
  8.9 5.2 %collective-permute-start.2 = (f32[16,128]{1,0:T(8,128)S(1)}, f32[16,128]{1,0:T(8,128)S(1)}, u32[]{:S(2)}, u32[]{:S(2)}) collective-permute-start(f32[16,128]{1,0:T(8,128)S(1)} %get-tuple-element.25), channel_id=1, source_target_pairs={{0,64},{64,0},{1,65},{65,1},{2,66},{66,2},{3,67},{67,3},{4,68},{68... | collective-permute-start | bytes 24584 | tf_op jit(solution)/shard_map/ppermute | solution.py:495
  15.3 4.0 %collective-permute-start.3 = (f32[32,128]{1,0:T(8,128)S(1)}, f32[32,128]{1,0:T(8,128)S(1)}, u32[]{:S(2)}, u32[]{:S(2)}) collective-permute-start(f32[32,128]{1,0:T(8,128)S(1)} %get-tuple-element.29), channel_id=1, source_target_pairs={{0,1},{1,0},{2,3},{3,2},{4,5},{5,4},{6,7},{7,6},{8,9},{9,8},{10,11... | collective-permute-start | bytes 49160 | tf_op jit(solution)/shard_map/ppermute | solution.py:479
  15.3 6.3 %collective-permute-start.4 = (f32[32,128]{1,0:T(8,128)S(1)}, f32[32,128]{1,0:T(8,128)S(1)}, u32[]{:S(2)}, u32[]{:S(2)}) collective-permute-start(f32[32,128]{1,0:T(8,128)S(1)} %get-tuple-element.34), channel_id=1, source_target_pairs={{0,64},{1,2},{2,1},{3,4},{4,3},{5,6},{6,5},{7,8},{8,7},{9,10},{10,... | collective-permute-start | bytes 49160 | tf_op jit(solution)/shard_map/ppermute | solution.py:491
  16.4 5.2 %collective-permute-start.5 = (f32[32,128]{1,0:T(8,128)S(1)}, f32[32,128]{1,0:T(8,128)S(1)}, u32[]{:S(2)}, u32[]{:S(2)}) collective-permute-start(f32[32,128]{1,0:T(8,128)S(1)} %get-tuple-element.35), channel_id=1, source_target_pairs={{0,64},{64,0},{1,65},{65,1},{2,66},{66,2},{3,67},{67,3},{4,68},{68... | collective-permute-start | bytes 49160 | tf_op jit(solution)/shard_map/ppermute | solution.py:495

commit v4 on v3

--- a/solution.py
+++ b/solution.py
@@ -327,19 +327,15 @@
     return sum_of([columns[k] * right[k : k + 1, :] for k in range(D)])
 
 
-def inverse_root(power, eye):
-    inverse = None
+def inverse_root(power, carried):
     for step in range(NS_STEPS):
-        if inverse is None:
-            following = 1.5 * eye - 0.5 * power
         columns = columns_of(power)
-        if inverse is not None:
-            following = 1.5 * inverse - 0.5 * times(columns, inverse)
+        following = [1.5 * pack - 0.5 * times(columns, pack) for pack in carried]
         if step < NS_STEPS - 1:
             square = times(columns, power)
             power = 2.25 * power - 1.5 * square + 0.25 * times(columns, square)
-        inverse = following
-    return inverse
+        carried = following
+    return carried
 
 
 def bond_weights(both, both_twist, edge_lanes):
@@ -360,15 +356,15 @@
     squares = jnp.broadcast_to(squares, (D, WIDE))
     trace = dot_split(squares, where_ones(inside)) + epsilon
     identity = jnp.where(iota((D, WIDE), 0) == minor(iota((D, WIDE), 1)), 1.0, 0.0)
-    inverse = inverse_root(gram / trace, identity).astype(bf16).astype(f32)
     spread = where_ones(iota((D, WIDE), 0) == minor(iota((D, WIDE), 1)))
     top_t, bottom_t = (packed(dot_first(half.astype(bf16), spread)) for half in (top, bottom))
-    columns = columns_of(inverse)
+    inverse, top_t, bottom_t = inverse_root(gram / trace, [identity, top_t, bottom_t])
+    inverse = inverse.astype(bf16).astype(f32)
     root = 1.0 / jnp.sqrt(trace)
     results = []
     for q_top, q_bottom in (
         (times(columns_of(top), inverse), times(columns_of(bottom), inverse)),
-        (times(columns, top_t), times(columns, bottom_t)),
+        (top_t, bottom_t),
     ):
         first = math.sqrt(weight_zero) * (q_top * root)
         second = math.sqrt(weight_one) * (q_bottom * root)

time: 24.6 us -> 24.6 us (level)
  transfers between devices with their start and end apart: 6 -> 6, of which waited for: 2 -> 2; matrix products, arithmetic and copies ran while one was open for 0% -> 0% of each run, Pallas kernels for 10% -> 9%
where the time goes in v4:
time: 24.6 us; the launch traced here: 24.4 us
  starting transfers between devices  12.4 us (50%)
  Pallas kernels  9.06 us (37%)
  waiting for transfers between devices  2.27 us (9%)
  between operations  0.68 us (3%)
    ppermute x2, starting transfers between devices, swap_far(): return lax.ppermute(value, ('group', 'tile'), pairs)  6.43 us
    ppermute x2, starting transfers between devices, swap_side(): return lax.ppermute(value, 'group', [(0, 1), (1, 0)])  5.8 us
    pallas_call x1, Pallas kernels, per_device(): call(last_kernel, [flat, messages], scratch, out_specs=in_hbm)  2.81 us
    pallas_call x1, Pallas kernels, per_device(): call(first_kernel, [((2, *tensor[0]), bf16), pack, pack, pack, pack, pack...  2.71 us
    pallas_call x1, Pallas kernels, per_device(): call(early_kernel, [tensor, spread, inner])(forms, near, received[0])  1.68 us
    ppermute x2, waiting for transfers between devices, swap_side(): return lax.ppermute(value, 'group', [(0, 1), (1, 0)])  1.6 us
    pallas_call x1, Pallas kernels, per_device(): call(second_kernel, [packs] * 5)(forms, edges, own, *received, *ahead)  1.23 us
    ppermute x2, waiting for transfers between devices, swap_far(): return lax.ppermute(value, ('group', 'tile'), pairs)  0.66 us
  transfers between devices with their start and end apart: 6, of which 2 were waited for; matrix products, arithmetic and copies ran while one was open for 0% of the time, Pallas kernels for 9%

profile of v4, /device:TPU:6, one launch (start us, length us, event | category | flops | bytes accessed | tf_op | source)
XLA Modules:
  0.0 24.4 jit_solution(6060203090491748696)
XLA Ops:
  0.6 2.7 %shard_map.41 = (bf16[2,3,2,256,256]{4,3,2,1,0:T(8,128)(2,1)S(1)}, f32[16,128]{1,0:T(8,128)S(1)}, f32[16,128]{1,0:T(8,128)S(1)}, f32[16,128]{1,0:T(8,128)S(1)}, ...) custom-call(bf16[3,1024,128]{2,1,0:T(8,128)(2,1)} %bitcast.12, f32[3,4,256]{2,1,0:T(4,128)} %bitcast.13), custom_call_target="tpu_custom_call" | custom-call | tf_op jit(solution)/shard_map/pallas_call | solution.py:515
  3.3 0.1 collective-permute-start
  3.4 5.4 %collective-permute-start.1 = (f32[16,128]{1,0:T(8,128)S(1)}, f32[16,128]{1,0:T(8,128)S(1)}, u32[]{:S(2)}, u32[]{:S(2)}) collective-permute-start(f32[16,128]{1,0:T(8,128)S(1)} %get-tuple-element.24), channel_id=1, source_target_pairs={{0,64},{1,2},{2,1},{3,4},{4,3},{5,6},{6,5},{7,8},{8,7},{9,10},{10,... | collective-permute-start | bytes 24584 | tf_op jit(solution)/shard_map/ppermute | solution.py:487
  8.9 2.9 %collective-permute-start.2 = (f32[16,128]{1,0:T(8,128)S(1)}, f32[16,128]{1,0:T(8,128)S(1)}, u32[]{:S(2)}, u32[]{:S(2)}) collective-permute-start(f32[16,128]{1,0:T(8,128)S(1)} %get-tuple-element.25), channel_id=1, source_target_pairs={{0,64},{64,0},{1,65},{65,1},{2,66},{66,2},{3,67},{67,3},{4,68},{68... | collective-permute-start | bytes 24584 | tf_op jit(solution)/shard_map/ppermute | solution.py:491
  11.8 0.0 collective-permute-done.near_in
  11.8 0.6 %shard_map.42 = (f32[2,2,256,256]{3,2,1,0:T(8,128)S(1)}, f32[2,2,16,256]{3,2,1,0:T(8,128)S(1)}) custom-call(bf16[2,3,2,256,256]{4,3,2,1,0:T(8,128)(2,1)S(1)} %get-tuple-element.20.form_ref, f32[16,128]{1,0:T(8,128)S(1)} %get-tuple-element.21.edge_ref, f32[16,128]{1,0:T(8,128)S(1)} %get-tuple-element.22.near_own, f32[16,128]{1,0:T(8,128)S(1)} %collective-permute-done.near_in), custom_call_target="tpu_custom_call" | custom-call | tf_op jit(solution)/shard_map/pallas_call | solution.py:519
  12.4 0.0 collective-permute-done.1.far_in
  12.4 1.6 %collective-permute-done.2.side_in = f32[16,128]{1,0:T(8,128)S(1)} collective-permute-done((f32[16,128]{1,0:T(8,128)S(1)}, f32[16,128]{1,0:T(8,128)S(1)}, u32[]{:S(2)}, u32[]{:S(2)}) %collective-permute-start.2) | collective-permute-done | bytes 8224 | tf_op jit(solution)/shard_map/ppermute | solution.py:491
  14.0 1.2 %shard_map.43 = (f32[32,128]{1,0:T(8,128)S(1)}, f32[32,128]{1,0:T(8,128)S(1)}, f32[32,128]{1,0:T(8,128)S(1)}, f32[32,128]{1,0:T(8,128)S(1)}, f32[32,128]{1,0:T(8,128)S(1)}) custom-call(bf16[2,3,2,256,256]{4,3,2,1,0:T(8,128)(2,1)S(1)} %get-tuple-element.20.form_ref, f32[16,128]{1,0:T(8,128)S(1)} %get-tuple-element.21.edge_ref, ...), custom_call_target="tpu_custom_call" | custom-call | tf_op jit(solution)/shard_map/pallas_call | solution.py:522
  15.3 0.1 collective-permute-start.3
  15.3 1.0 %collective-permute-start.4 = (f32[32,128]{1,0:T(8,128)S(1)}, f32[32,128]{1,0:T(8,128)S(1)}, u32[]{:S(2)}, u32[]{:S(2)}) collective-permute-start(f32[32,128]{1,0:T(8,128)S(1)} %get-tuple-element.34), channel_id=1, source_target_pairs={{0,64},{1,2},{2,1},{3,4},{4,3},{5,6},{6,5},{7,8},{8,7},{9,10},{10,... | collective-permute-start | bytes 49160 | tf_op jit(solution)/shard_map/ppermute | solution.py:487
  16.4 2.9 %collective-permute-start.5 = (f32[32,128]{1,0:T(8,128)S(1)}, f32[32,128]{1,0:T(8,128)S(1)}, u32[]{:S(2)}, u32[]{:S(2)}) collective-permute-start(f32[32,128]{1,0:T(8,128)S(1)} %get-tuple-element.35), channel_id=1, source_target_pairs={{0,64},{64,0},{1,65},{65,1},{2,66},{66,2},{3,67},{67,3},{4,68},{68... | collective-permute-start | bytes 49160 | tf_op jit(solution)/shard_map/ppermute | solution.py:491
  19.3 0.0 collective-permute-done.3.near_in
  19.3 1.7 %shard_map.44 = (bf16[3,2,256,256]{3,2,1,0:T(8,128)(2,1)S(1)}, bf16[2,3,16,256]{3,2,1,0:T(8,128)(2,1)S(1)}, bf16[2,2,2,16,256]{4,3,2,1,0:T(8,128)(2,1)S(1)}) custom-call(bf16[2,3,2,256,256]{4,3,2,1,0:T(8,128)(2,1)S(1)} %get-tuple-element.20.form_ref, f32[32,128]{1,0:T(8,128)S(1)} %get-tuple-element.28.near_own, f32[32,128]{1,0:T(8,128)S(1)} %collective-permute-done.3.near_in), custom_call_target="tpu_custom_call" | custom-call | tf_op jit(solution)/shard_map/pallas_call | solution.py:526
  20.9 0.7 %collective-permute-done.4.far_in = f32[32,128]{1,0:T(8,128)S(1)} collective-permute-done((f32[32,128]{1,0:T(8,128)S(1)}, f32[32,128]{1,0:T(8,128)S(1)}, u32[]{:S(2)}, u32[]{:S(2)}) %collective-permute-start.4) | collective-permute-done | bytes 16416 | tf_op jit(solution)/shard_map/ppermute | solution.py:487
  21.6 0.0 collective-permute-done.5.side_in
  21.6 2.8 %shard_map.45 = (bf16[3,1024,128]{2,1,0:T(8,128)(2,1)}, f32[3,4,256]{2,1,0:T(4,128)}) custom-call(bf16[3,2,256,256]{3,2,1,0:T(8,128)(2,1)S(1)} %get-tuple-element.30.gated_ref, bf16[2,3,16,256]{3,2,1,0:T(8,128)(2,1)S(1)} %get-tuple-element.31.near_ref, bf16[2,2,2,16,256]{4,3,2,1,0:T(8,128)(2,1)S(1)} %get-tuple-element.32.inner_ref, ...), custom_call_target="tpu_custom_call" | custom-call | tf_op jit(solution)/shard_map/pallas_call | solution.py:527
Async XLA Ops:
  3.3 8.4 %collective-permute-start = (f32[16,128]{1,0:T(8,128)S(1)}, f32[16,128]{1,0:T(8,128)S(1)}, u32[]{:S(2)}, u32[]{:S(2)}) collective-permute-start(f32[16,128]{1,0:T(8,128)S(1)} %get-tuple-element.23), channel_id=1, source_target_pairs={{0,1},{1,0},{2,3},{3,2},{4,5},{5,4},{6,7},{7,6},{8,9},{9,8},{10,11... | collective-permute-start | bytes 24584 | tf_op jit(solution)/shard_map/ppermute | solution.py:475
  3.4 9.0 %collective-permute-start.1 = (f32[16,128]{1,0:T(8,128)S(1)}, f32[16,128]{1,0:T(8,128)S(1)}, u32[]{:S(2)}, u32[]{:S(2)}) collective-permute-start(f32[16,128]{1,0:T(8,128)S(1)} %get-tuple-element.24), channel_id=1, source_target_pairs={{0,64},{1,2},{2,1},{3,4},{4,3},{5,6},{6,5},{7,8},{8,7},{9,10},{10,... | collective-permute-start | bytes 24584 | tf_op jit(solution)/shard_map/ppermute | solution.py:487
  8.9 5.2 %collective-permute-start.2 = (f32[16,128]{1,0:T(8,128)S(1)}, f32[16,128]{1,0:T(8,128)S(1)}, u32[]{:S(2)}, u32[]{:S(2)}) collective-permute-start(f32[16,128]{1,0:T(8,128)S(1)} %get-tuple-element.25), channel_id=1, source_target_pairs={{0,64},{64,0},{1,65},{65,1},{2,66},{66,2},{3,67},{67,3},{4,68},{68... | collective-permute-start | bytes 24584 | tf_op jit(solution)/shard_map/ppermute | solution.py:491
  15.3 4.0 %collective-permute-start.3 = (f32[32,128]{1,0:T(8,128)S(1)}, f32[32,128]{1,0:T(8,128)S(1)}, u32[]{:S(2)}, u32[]{:S(2)}) collective-permute-start(f32[32,128]{1,0:T(8,128)S(1)} %get-tuple-element.29), channel_id=1, source_target_pairs={{0,1},{1,0},{2,3},{3,2},{4,5},{5,4},{6,7},{7,6},{8,9},{9,8},{10,11... | collective-permute-start | bytes 49160 | tf_op jit(solution)/shard_map/ppermute | solution.py:475
  15.3 6.3 %collective-permute-start.4 = (f32[32,128]{1,0:T(8,128)S(1)}, f32[32,128]{1,0:T(8,128)S(1)}, u32[]{:S(2)}, u32[]{:S(2)}) collective-permute-start(f32[32,128]{1,0:T(8,128)S(1)} %get-tuple-element.34), channel_id=1, source_target_pairs={{0,64},{1,2},{2,1},{3,4},{4,3},{5,6},{6,5},{7,8},{8,7},{9,10},{10,... | collective-permute-start | bytes 49160 | tf_op jit(solution)/shard_map/ppermute | solution.py:487
  16.4 5.2 %collective-permute-start.5 = (f32[32,128]{1,0:T(8,128)S(1)}, f32[32,128]{1,0:T(8,128)S(1)}, u32[]{:S(2)}, u32[]{:S(2)}) collective-permute-start(f32[32,128]{1,0:T(8,128)S(1)} %get-tuple-element.35), channel_id=1, source_target_pairs={{0,64},{64,0},{1,65},{65,1},{2,66},{66,2},{3,67},{67,3},{4,68},{68... | collective-permute-start | bytes 49160 | tf_op jit(solution)/shard_map/ppermute | solution.py:491

commit v5 on v4

--- a/solution.py
+++ b/solution.py
@@ -124,7 +124,9 @@
         (1, down, right, up, left, DOWN, RIGHT),
     ):
         weight = kron(k_rep, k_tile)
-        full = product(x_ref, form, site, 0, weight) + product(x_ref, form, site, 1, weight)
+        kept = dot(x_ref[form, site].reshape(STATES * SQ, SQ), weight).astype(bf16)
+        kept = jnp.concatenate([kept[:SQ], kept[SQ:]], axis=1)
+        full = dot(kept, x_ref[1 - form, site].reshape(STATES * SQ, SQ))
         parts[leg_rep] = [fold_minor(full, m_tile)]
         parts[leg_tile] = [fold_major(full, m_rep)]
     return parts

time: 24.6 us -> 24.5 us (level)
  transfers between devices with their start and end apart: 6 -> 6, of which waited for: 2 -> 2; matrix products, arithmetic and copies ran while one was open for 0% -> 0% of each run, Pallas kernels for 9% -> 10%
where the time goes in v5:
time: 24.5 us; the launch traced here: 24.3 us
  starting transfers between devices  12.4 us (51%)
  Pallas kernels  8.98 us (37%)
  waiting for transfers between devices  2.27 us (9%)
  between operations  0.68 us (3%)
    ppermute x2, starting transfers between devices, swap_far(): return lax.ppermute(value, ('group', 'tile'), pairs)  6.43 us
    ppermute x2, starting transfers between devices, swap_side(): return lax.ppermute(value, 'group', [(0, 1), (1, 0)])  5.8 us
    pallas_call x1, Pallas kernels, per_device(): call(last_kernel, [flat, messages], scratch, out_specs=in_hbm)  2.81 us
    pallas_call x1, Pallas kernels, per_device(): call(first_kernel, [((2, *tensor[0]), bf16), pack, pack, pack, pack, pack...  2.62 us
    pallas_call x1, Pallas kernels, per_device(): call(early_kernel, [tensor, spread, inner])(forms, near, received[0])  1.68 us
    ppermute x2, waiting for transfers between devices, swap_side(): return lax.ppermute(value, 'group', [(0, 1), (1, 0)])  1.6 us
    pallas_call x1, Pallas kernels, per_device(): call(second_kernel, [packs] * 5)(forms, edges, own, *received, *ahead)  1.23 us
    ppermute x2, waiting for transfers between devices, swap_far(): return lax.ppermute(value, ('group', 'tile'), pairs)  0.66 us
  transfers between devices with their start and end apart: 6, of which 2 were waited for; matrix products, arithmetic and copies ran while one was open for 0% of the time, Pallas kernels for 10%

profile of v5, /device:TPU:6, one launch (start us, length us, event | category | flops | bytes accessed | tf_op | source)
XLA Modules:
  0.0 24.3 jit_solution(2307522928035622967)
XLA Ops:
  0.6 2.6 %shard_map.41 = (bf16[2,3,2,256,256]{4,3,2,1,0:T(8,128)(2,1)S(1)}, f32[16,128]{1,0:T(8,128)S(1)}, f32[16,128]{1,0:T(8,128)S(1)}, f32[16,128]{1,0:T(8,128)S(1)}, ...) custom-call(bf16[3,1024,128]{2,1,0:T(8,128)(2,1)} %bitcast.12, f32[3,4,256]{2,1,0:T(4,128)} %bitcast.13), custom_call_target="tpu_custom_call" | custom-call | tf_op jit(solution)/shard_map/pallas_call | solution.py:517
  3.3 0.1 collective-permute-start
  3.4 5.4 %collective-permute-start.1 = (f32[16,128]{1,0:T(8,128)S(1)}, f32[16,128]{1,0:T(8,128)S(1)}, u32[]{:S(2)}, u32[]{:S(2)}) collective-permute-start(f32[16,128]{1,0:T(8,128)S(1)} %get-tuple-element.24), channel_id=1, source_target_pairs={{0,64},{1,2},{2,1},{3,4},{4,3},{5,6},{6,5},{7,8},{8,7},{9,10},{10,... | collective-permute-start | bytes 24584 | tf_op jit(solution)/shard_map/ppermute | solution.py:489
  8.8 2.9 %collective-permute-start.2 = (f32[16,128]{1,0:T(8,128)S(1)}, f32[16,128]{1,0:T(8,128)S(1)}, u32[]{:S(2)}, u32[]{:S(2)}) collective-permute-start(f32[16,128]{1,0:T(8,128)S(1)} %get-tuple-element.25), channel_id=1, source_target_pairs={{0,64},{64,0},{1,65},{65,1},{2,66},{66,2},{3,67},{67,3},{4,68},{68... | collective-permute-start | bytes 24584 | tf_op jit(solution)/shard_map/ppermute | solution.py:493
  11.7 0.0 collective-permute-done.near_in
  11.7 0.6 %shard_map.42 = (f32[2,2,256,256]{3,2,1,0:T(8,128)S(1)}, f32[2,2,16,256]{3,2,1,0:T(8,128)S(1)}) custom-call(bf16[2,3,2,256,256]{4,3,2,1,0:T(8,128)(2,1)S(1)} %get-tuple-element.20.form_ref, f32[16,128]{1,0:T(8,128)S(1)} %get-tuple-element.21.edge_ref, f32[16,128]{1,0:T(8,128)S(1)} %get-tuple-element.22.near_own, f32[16,128]{1,0:T(8,128)S(1)} %collective-permute-done.near_in), custom_call_target="tpu_custom_call" | custom-call | tf_op jit(solution)/shard_map/pallas_call | solution.py:521
  12.3 0.0 collective-permute-done.1.far_in
  12.3 1.6 %collective-permute-done.2.side_in = f32[16,128]{1,0:T(8,128)S(1)} collective-permute-done((f32[16,128]{1,0:T(8,128)S(1)}, f32[16,128]{1,0:T(8,128)S(1)}, u32[]{:S(2)}, u32[]{:S(2)}) %collective-permute-start.2) | collective-permute-done | bytes 8224 | tf_op jit(solution)/shard_map/ppermute | solution.py:493
  13.9 1.2 %shard_map.43 = (f32[32,128]{1,0:T(8,128)S(1)}, f32[32,128]{1,0:T(8,128)S(1)}, f32[32,128]{1,0:T(8,128)S(1)}, f32[32,128]{1,0:T(8,128)S(1)}, f32[32,128]{1,0:T(8,128)S(1)}) custom-call(bf16[2,3,2,256,256]{4,3,2,1,0:T(8,128)(2,1)S(1)} %get-tuple-element.20.form_ref, f32[16,128]{1,0:T(8,128)S(1)} %get-tuple-element.21.edge_ref, ...), custom_call_target="tpu_custom_call" | custom-call | tf_op jit(solution)/shard_map/pallas_call | solution.py:524
  15.2 0.1 collective-permute-start.3
  15.3 1.0 %collective-permute-start.4 = (f32[32,128]{1,0:T(8,128)S(1)}, f32[32,128]{1,0:T(8,128)S(1)}, u32[]{:S(2)}, u32[]{:S(2)}) collective-permute-start(f32[32,128]{1,0:T(8,128)S(1)} %get-tuple-element.34), channel_id=1, source_target_pairs={{0,64},{1,2},{2,1},{3,4},{4,3},{5,6},{6,5},{7,8},{8,7},{9,10},{10,... | collective-permute-start | bytes 49160 | tf_op jit(solution)/shard_map/ppermute | solution.py:489
  16.3 2.9 %collective-permute-start.5 = (f32[32,128]{1,0:T(8,128)S(1)}, f32[32,128]{1,0:T(8,128)S(1)}, u32[]{:S(2)}, u32[]{:S(2)}) collective-permute-start(f32[32,128]{1,0:T(8,128)S(1)} %get-tuple-element.35), channel_id=1, source_target_pairs={{0,64},{64,0},{1,65},{65,1},{2,66},{66,2},{3,67},{67,3},{4,68},{68... | collective-permute-start | bytes 49160 | tf_op jit(solution)/shard_map/ppermute | solution.py:493
  19.2 0.0 collective-permute-done.3.near_in
  19.2 1.7 %shard_map.44 = (bf16[3,2,256,256]{3,2,1,0:T(8,128)(2,1)S(1)}, bf16[2,3,16,256]{3,2,1,0:T(8,128)(2,1)S(1)}, bf16[2,2,2,16,256]{4,3,2,1,0:T(8,128)(2,1)S(1)}) custom-call(bf16[2,3,2,256,256]{4,3,2,1,0:T(8,128)(2,1)S(1)} %get-tuple-element.20.form_ref, f32[32,128]{1,0:T(8,128)S(1)} %get-tuple-element.28.near_own, f32[32,128]{1,0:T(8,128)S(1)} %collective-permute-done.3.near_in), custom_call_target="tpu_custom_call" | custom-call | tf_op jit(solution)/shard_map/pallas_call | solution.py:528
  20.9 0.7 %collective-permute-done.4.far_in = f32[32,128]{1,0:T(8,128)S(1)} collective-permute-done((f32[32,128]{1,0:T(8,128)S(1)}, f32[32,128]{1,0:T(8,128)S(1)}, u32[]{:S(2)}, u32[]{:S(2)}) %collective-permute-start.4) | collective-permute-done | bytes 16416 | tf_op jit(solution)/shard_map/ppermute | solution.py:489
  21.5 0.0 collective-permute-done.5.side_in
  21.5 2.8 %shard_map.45 = (bf16[3,1024,128]{2,1,0:T(8,128)(2,1)}, f32[3,4,256]{2,1,0:T(4,128)}) custom-call(bf16[3,2,256,256]{3,2,1,0:T(8,128)(2,1)S(1)} %get-tuple-element.30.gated_ref, bf16[2,3,16,256]{3,2,1,0:T(8,128)(2,1)S(1)} %get-tuple-element.31.near_ref, bf16[2,2,2,16,256]{4,3,2,1,0:T(8,128)(2,1)S(1)} %get-tuple-element.32.inner_ref, ...), custom_call_target="tpu_custom_call" | custom-call | tf_op jit(solution)/shard_map/pallas_call | solution.py:529
Async XLA Ops:
  3.3 8.4 %collective-permute-start = (f32[16,128]{1,0:T(8,128)S(1)}, f32[16,128]{1,0:T(8,128)S(1)}, u32[]{:S(2)}, u32[]{:S(2)}) collective-permute-start(f32[16,128]{1,0:T(8,128)S(1)} %get-tuple-element.23), channel_id=1, source_target_pairs={{0,1},{1,0},{2,3},{3,2},{4,5},{5,4},{6,7},{7,6},{8,9},{9,8},{10,11... | collective-permute-start | bytes 24584 | tf_op jit(solution)/shard_map/ppermute | solution.py:477
  3.4 9.0 %collective-permute-start.1 = (f32[16,128]{1,0:T(8,128)S(1)}, f32[16,128]{1,0:T(8,128)S(1)}, u32[]{:S(2)}, u32[]{:S(2)}) collective-permute-start(f32[16,128]{1,0:T(8,128)S(1)} %get-tuple-element.24), channel_id=1, source_target_pairs={{0,64},{1,2},{2,1},{3,4},{4,3},{5,6},{6,5},{7,8},{8,7},{9,10},{10,... | collective-permute-start | bytes 24584 | tf_op jit(solution)/shard_map/ppermute | solution.py:489
  8.8 5.2 %collective-permute-start.2 = (f32[16,128]{1,0:T(8,128)S(1)}, f32[16,128]{1,0:T(8,128)S(1)}, u32[]{:S(2)}, u32[]{:S(2)}) collective-permute-start(f32[16,128]{1,0:T(8,128)S(1)} %get-tuple-element.25), channel_id=1, source_target_pairs={{0,64},{64,0},{1,65},{65,1},{2,66},{66,2},{3,67},{67,3},{4,68},{68... | collective-permute-start | bytes 24584 | tf_op jit(solution)/shard_map/ppermute | solution.py:493
  15.2 4.0 %collective-permute-start.3 = (f32[32,128]{1,0:T(8,128)S(1)}, f32[32,128]{1,0:T(8,128)S(1)}, u32[]{:S(2)}, u32[]{:S(2)}) collective-permute-start(f32[32,128]{1,0:T(8,128)S(1)} %get-tuple-element.29), channel_id=1, source_target_pairs={{0,1},{1,0},{2,3},{3,2},{4,5},{5,4},{6,7},{7,6},{8,9},{9,8},{10,11... | collective-permute-start | bytes 49160 | tf_op jit(solution)/shard_map/ppermute | solution.py:477
  15.3 6.3 %collective-permute-start.4 = (f32[32,128]{1,0:T(8,128)S(1)}, f32[32,128]{1,0:T(8,128)S(1)}, u32[]{:S(2)}, u32[]{:S(2)}) collective-permute-start(f32[32,128]{1,0:T(8,128)S(1)} %get-tuple-element.34), channel_id=1, source_target_pairs={{0,64},{1,2},{2,1},{3,4},{4,3},{5,6},{6,5},{7,8},{8,7},{9,10},{10,... | collective-permute-start | bytes 49160 | tf_op jit(solution)/shard_map/ppermute | solution.py:489
  16.3 5.2 %collective-permute-start.5 = (f32[32,128]{1,0:T(8,128)S(1)}, f32[32,128]{1,0:T(8,128)S(1)}, u32[]{:S(2)}, u32[]{:S(2)}) collective-permute-start(f32[32,128]{1,0:T(8,128)S(1)} %get-tuple-element.35), channel_id=1, source_target_pairs={{0,64},{64,0},{1,65},{65,1},{2,66},{66,2},{3,67},{67,3},{4,68},{68... | collective-permute-start | bytes 49160 | tf_op jit(solution)/shard_map/ppermute | solution.py:493

commit v6 on v5

--- a/solution.py
+++ b/solution.py
@@ -444,8 +444,8 @@
             ups, downs, lefts, rights = factors[s]
             upper = kron(ups[site], lefts[site])
             lower = kron(downs[site], rights[site])
-            gated = dot(upper, gated_ref[site, s]).astype(bf16)
-            gated = dot(gated, lower)
+            gated = dot(gated_ref[site, s], lower).astype(bf16)
+            gated = dot(upper, gated)
             for half in range(2):
                 lanes = gated[:, half * 128 : half * 128 + 128]
                 wide_ref[site, pl.ds(2 * half + s, SQ, stride=4), :] = lanes

time: 24.5 us -> 24.6 us (level)
  transfers between devices with their start and end apart: 6 -> 6, of which waited for: 2 -> 2; matrix products, arithmetic and copies ran while one was open for 0% -> 0% of each run, Pallas kernels for 10% -> 9%
where the time goes in v6:
time: 24.6 us; the launch traced here: 24.4 us
  starting transfers between devices  12.4 us (50%)
  Pallas kernels  9.07 us (37%)
  waiting for transfers between devices  2.27 us (9%)
  between operations  0.68 us (3%)
    ppermute x2, starting transfers between devices, swap_far(): return lax.ppermute(value, ('group', 'tile'), pairs)  6.43 us
    ppermute x2, starting transfers between devices, swap_side(): return lax.ppermute(value, 'group', [(0, 1), (1, 0)])  5.8 us
    pallas_call x1, Pallas kernels, per_device(): call(last_kernel, [flat, messages], scratch, out_specs=in_hbm)  2.9 us
    pallas_call x1, Pallas kernels, per_device(): call(first_kernel, [((2, *tensor[0]), bf16), pack, pack, pack, pack, pack...  2.62 us
    pallas_call x1, Pallas kernels, per_device(): call(early_kernel, [tensor, spread, inner])(forms, near, received[0])  1.68 us
    ppermute x2, waiting for transfers between devices, swap_side(): return lax.ppermute(value, 'group', [(0, 1), (1, 0)])  1.6 us
    pallas_call x1, Pallas kernels, per_device(): call(second_kernel, [packs] * 5)(forms, edges, own, *received, *ahead)  1.23 us
    ppermute x2, waiting for transfers between devices, swap_far(): return lax.ppermute(value, ('group', 'tile'), pairs)  0.66 us
  transfers between devices with their start and end apart: 6, of which 2 were waited for; matrix products, arithmetic and copies ran while one was open for 0% of the time, Pallas kernels for 9%

profile of v6, /device:TPU:6, one launch (start us, length us, event | category | flops | bytes accessed | tf_op | source)
XLA Modules:
  0.0 24.4 jit_solution(3021769243931412830)
XLA Ops:
  0.6 2.6 %shard_map.41 = (bf16[2,3,2,256,256]{4,3,2,1,0:T(8,128)(2,1)S(1)}, f32[16,128]{1,0:T(8,128)S(1)}, f32[16,128]{1,0:T(8,128)S(1)}, f32[16,128]{1,0:T(8,128)S(1)}, ...) custom-call(bf16[3,1024,128]{2,1,0:T(8,128)(2,1)} %bitcast.12, f32[3,4,256]{2,1,0:T(4,128)} %bitcast.13), custom_call_target="tpu_custom_call" | custom-call | tf_op jit(solution)/shard_map/pallas_call | solution.py:517
  3.3 0.1 collective-permute-start
  3.4 5.4 %collective-permute-start.1 = (f32[16,128]{1,0:T(8,128)S(1)}, f32[16,128]{1,0:T(8,128)S(1)}, u32[]{:S(2)}, u32[]{:S(2)}) collective-permute-start(f32[16,128]{1,0:T(8,128)S(1)} %get-tuple-element.24), channel_id=1, source_target_pairs={{0,64},{1,2},{2,1},{3,4},{4,3},{5,6},{6,5},{7,8},{8,7},{9,10},{10,... | collective-permute-start | bytes 24584 | tf_op jit(solution)/shard_map/ppermute | solution.py:489
  8.8 2.9 %collective-permute-start.2 = (f32[16,128]{1,0:T(8,128)S(1)}, f32[16,128]{1,0:T(8,128)S(1)}, u32[]{:S(2)}, u32[]{:S(2)}) collective-permute-start(f32[16,128]{1,0:T(8,128)S(1)} %get-tuple-element.25), channel_id=1, source_target_pairs={{0,64},{64,0},{1,65},{65,1},{2,66},{66,2},{3,67},{67,3},{4,68},{68... | collective-permute-start | bytes 24584 | tf_op jit(solution)/shard_map/ppermute | solution.py:493
  11.7 0.0 collective-permute-done.near_in
  11.7 0.6 %shard_map.42 = (f32[2,2,256,256]{3,2,1,0:T(8,128)S(1)}, f32[2,2,16,256]{3,2,1,0:T(8,128)S(1)}) custom-call(bf16[2,3,2,256,256]{4,3,2,1,0:T(8,128)(2,1)S(1)} %get-tuple-element.20.form_ref, f32[16,128]{1,0:T(8,128)S(1)} %get-tuple-element.21.edge_ref, f32[16,128]{1,0:T(8,128)S(1)} %get-tuple-element.22.near_own, f32[16,128]{1,0:T(8,128)S(1)} %collective-permute-done.near_in), custom_call_target="tpu_custom_call" | custom-call | tf_op jit(solution)/shard_map/pallas_call | solution.py:521
  12.3 0.0 collective-permute-done.1.far_in
  12.3 1.6 %collective-permute-done.2.side_in = f32[16,128]{1,0:T(8,128)S(1)} collective-permute-done((f32[16,128]{1,0:T(8,128)S(1)}, f32[16,128]{1,0:T(8,128)S(1)}, u32[]{:S(2)}, u32[]{:S(2)}) %collective-permute-start.2) | collective-permute-done | bytes 8224 | tf_op jit(solution)/shard_map/ppermute | solution.py:493
  13.9 1.2 %shard_map.43 = (f32[32,128]{1,0:T(8,128)S(1)}, f32[32,128]{1,0:T(8,128)S(1)}, f32[32,128]{1,0:T(8,128)S(1)}, f32[32,128]{1,0:T(8,128)S(1)}, f32[32,128]{1,0:T(8,128)S(1)}) custom-call(bf16[2,3,2,256,256]{4,3,2,1,0:T(8,128)(2,1)S(1)} %get-tuple-element.20.form_ref, f32[16,128]{1,0:T(8,128)S(1)} %get-tuple-element.21.edge_ref, ...), custom_call_target="tpu_custom_call" | custom-call | tf_op jit(solution)/shard_map/pallas_call | solution.py:524
  15.2 0.1 collective-permute-start.3
  15.3 1.0 %collective-permute-start.4 = (f32[32,128]{1,0:T(8,128)S(1)}, f32[32,128]{1,0:T(8,128)S(1)}, u32[]{:S(2)}, u32[]{:S(2)}) collective-permute-start(f32[32,128]{1,0:T(8,128)S(1)} %get-tuple-element.34), channel_id=1, source_target_pairs={{0,64},{1,2},{2,1},{3,4},{4,3},{5,6},{6,5},{7,8},{8,7},{9,10},{10,... | collective-permute-start | bytes 49160 | tf_op jit(solution)/shard_map/ppermute | solution.py:489
  16.3 2.9 %collective-permute-start.5 = (f32[32,128]{1,0:T(8,128)S(1)}, f32[32,128]{1,0:T(8,128)S(1)}, u32[]{:S(2)}, u32[]{:S(2)}) collective-permute-start(f32[32,128]{1,0:T(8,128)S(1)} %get-tuple-element.35), channel_id=1, source_target_pairs={{0,64},{64,0},{1,65},{65,1},{2,66},{66,2},{3,67},{67,3},{4,68},{68... | collective-permute-start | bytes 49160 | tf_op jit(solution)/shard_map/ppermute | solution.py:493
  19.2 0.0 collective-permute-done.3.near_in
  19.2 1.7 %shard_map.44 = (bf16[3,2,256,256]{3,2,1,0:T(8,128)(2,1)S(1)}, bf16[2,3,16,256]{3,2,1,0:T(8,128)(2,1)S(1)}, bf16[2,2,2,16,256]{4,3,2,1,0:T(8,128)(2,1)S(1)}) custom-call(bf16[2,3,2,256,256]{4,3,2,1,0:T(8,128)(2,1)S(1)} %get-tuple-element.20.form_ref, f32[32,128]{1,0:T(8,128)S(1)} %get-tuple-element.28.near_own, f32[32,128]{1,0:T(8,128)S(1)} %collective-permute-done.3.near_in), custom_call_target="tpu_custom_call" | custom-call | tf_op jit(solution)/shard_map/pallas_call | solution.py:528
  20.9 0.7 %collective-permute-done.4.far_in = f32[32,128]{1,0:T(8,128)S(1)} collective-permute-done((f32[32,128]{1,0:T(8,128)S(1)}, f32[32,128]{1,0:T(8,128)S(1)}, u32[]{:S(2)}, u32[]{:S(2)}) %collective-permute-start.4) | collective-permute-done | bytes 16416 | tf_op jit(solution)/shard_map/ppermute | solution.py:489
  21.5 0.0 collective-permute-done.5.side_in
  21.5 2.9 %shard_map.45 = (bf16[3,1024,128]{2,1,0:T(8,128)(2,1)}, f32[3,4,256]{2,1,0:T(4,128)}) custom-call(bf16[3,2,256,256]{3,2,1,0:T(8,128)(2,1)S(1)} %get-tuple-element.30.gated_ref, bf16[2,3,16,256]{3,2,1,0:T(8,128)(2,1)S(1)} %get-tuple-element.31.near_ref, bf16[2,2,2,16,256]{4,3,2,1,0:T(8,128)(2,1)S(1)} %get-tuple-element.32.inner_ref, ...), custom_call_target="tpu_custom_call" | custom-call | tf_op jit(solution)/shard_map/pallas_call | solution.py:529
Async XLA Ops:
  3.3 8.4 %collective-permute-start = (f32[16,128]{1,0:T(8,128)S(1)}, f32[16,128]{1,0:T(8,128)S(1)}, u32[]{:S(2)}, u32[]{:S(2)}) collective-permute-start(f32[16,128]{1,0:T(8,128)S(1)} %get-tuple-element.23), channel_id=1, source_target_pairs={{0,1},{1,0},{2,3},{3,2},{4,5},{5,4},{6,7},{7,6},{8,9},{9,8},{10,11... | collective-permute-start | bytes 24584 | tf_op jit(solution)/shard_map/ppermute | solution.py:477
  3.4 9.0 %collective-permute-start.1 = (f32[16,128]{1,0:T(8,128)S(1)}, f32[16,128]{1,0:T(8,128)S(1)}, u32[]{:S(2)}, u32[]{:S(2)}) collective-permute-start(f32[16,128]{1,0:T(8,128)S(1)} %get-tuple-element.24), channel_id=1, source_target_pairs={{0,64},{1,2},{2,1},{3,4},{4,3},{5,6},{6,5},{7,8},{8,7},{9,10},{10,... | collective-permute-start | bytes 24584 | tf_op jit(solution)/shard_map/ppermute | solution.py:489
  8.8 5.2 %collective-permute-start.2 = (f32[16,128]{1,0:T(8,128)S(1)}, f32[16,128]{1,0:T(8,128)S(1)}, u32[]{:S(2)}, u32[]{:S(2)}) collective-permute-start(f32[16,128]{1,0:T(8,128)S(1)} %get-tuple-element.25), channel_id=1, source_target_pairs={{0,64},{64,0},{1,65},{65,1},{2,66},{66,2},{3,67},{67,3},{4,68},{68... | collective-permute-start | bytes 24584 | tf_op jit(solution)/shard_map/ppermute | solution.py:493
  15.2 4.0 %collective-permute-start.3 = (f32[32,128]{1,0:T(8,128)S(1)}, f32[32,128]{1,0:T(8,128)S(1)}, u32[]{:S(2)}, u32[]{:S(2)}) collective-permute-start(f32[32,128]{1,0:T(8,128)S(1)} %get-tuple-element.29), channel_id=1, source_target_pairs={{0,1},{1,0},{2,3},{3,2},{4,5},{5,4},{6,7},{7,6},{8,9},{9,8},{10,11... | collective-permute-start | bytes 49160 | tf_op jit(solution)/shard_map/ppermute | solution.py:477
  15.3 6.3 %collective-permute-start.4 = (f32[32,128]{1,0:T(8,128)S(1)}, f32[32,128]{1,0:T(8,128)S(1)}, u32[]{:S(2)}, u32[]{:S(2)}) collective-permute-start(f32[32,128]{1,0:T(8,128)S(1)} %get-tuple-element.34), channel_id=1, source_target_pairs={{0,64},{1,2},{2,1},{3,4},{4,3},{5,6},{6,5},{7,8},{8,7},{9,10},{10,... | collective-permute-start | bytes 49160 | tf_op jit(solution)/shard_map/ppermute | solution.py:489
  16.3 5.2 %collective-permute-start.5 = (f32[32,128]{1,0:T(8,128)S(1)}, f32[32,128]{1,0:T(8,128)S(1)}, u32[]{:S(2)}, u32[]{:S(2)}) collective-permute-start(f32[32,128]{1,0:T(8,128)S(1)} %get-tuple-element.35), channel_id=1, source_target_pairs={{0,64},{64,0},{1,65},{65,1},{2,66},{66,2},{3,67},{67,3},{4,68},{68... | collective-permute-start | bytes 49160 | tf_op jit(solution)/shard_map/ppermute | solution.py:493
